TPU v7x, 1024 devices: a whole 4x8x16 slice. The times are simulated.
1024 devices in a mesh: expert: 32 (over z, y_hi), dp: 32 (over y_lo, x, core).
Axes of the slice: x: 4, y: 8 (y_hi: 2, y_lo: 4; y = y_hi * 4 + y_lo), z: 16, core: 2. Of those that a mesh axis runs over, the one named last changes fastest.
Arguments:
- tokens: bfloat16 [131072, 2560], P(('expert', 'dp')), may hold values from -24 to 24
- cotangent: bfloat16 [131072, 2560], P(('expert', 'dp')), may hold values from -0.09375 to 0.09375
- route_weight: float32 [131072], P(('expert', 'dp')), may hold values from 0.1 to 1
- expert_ids: int32 [131072, 1], P(('expert', 'dp')), may hold values from 0 to 31; in each aligned block of 128 rows (0 to 127, 128 to 255, ...) at most 6 rows name the same one
- dense_gate: bfloat16 [2560, 4096], P('dp', 'expert'), may hold values from -0.125 to 0.125
- dense_up: bfloat16 [2560, 4096], P('dp', 'expert'), may hold values from -0.125 to 0.125
- dense_down_t: bfloat16 [2560, 4096], P('dp', 'expert'), may hold values from -0.5 to 0.5
- seed_map: int32 [32], replicated, may hold values from 0 to 31, as said below
Outputs:
- expert_grads: float32 [32, 2560, 384], P('expert', 'dp')
Inputs may be any that keep to these rules, and one draw needn't show every extreme that they name: `expert_ids`: among the 128 tokens of one device no expert is named more than 6 times, a bound that some block reaches. `seed_map`: each expert names one dense slice; several experts may name the same one.
All inputs are finite; a program needn't handle non-finite values.
Results may differ from a plain program's by a relative error of at most 0.0041.
Values may be sent and summed in bfloat16 or wider, within the bound.
No kernel may reach another device: no remote copies, remote signals or barrier semaphores. Data moves between devices by JAX's collectives and lax.ppermute only.
A program may use at most 32 MiB of HBM per device.

v0:
```python
import jax
import jax.numpy as jnp
from jax import lax
from jax.sharding import PartitionSpec as P

TOP = 1


def contract_rows(first_operand, second_operand):
    return lax.dot_general(
        first_operand, second_operand, (((0,), (0,)), ((), ())), preferred_element_type=jnp.float32
    )


def activation_grads(joined, back_h):
    hidden = back_h.shape[1]
    pre_gate = joined[:, :hidden]
    pre_up = joined[:, hidden:]
    logistic = jax.nn.sigmoid(pre_gate)
    gated = pre_gate * logistic
    gate_slope = logistic * (1.0 + pre_gate * (1.0 - logistic))
    mixed_h = (gated * pre_up).astype(jnp.bfloat16)
    grad_pre = jnp.concatenate([back_h * pre_up * gate_slope, back_h * gated], axis=1).astype(
        jnp.bfloat16
    )
    return (mixed_h, grad_pre)


def weight_terms(row_x, row_g, grad_pre, mixed_h):
    return jnp.concatenate([contract_rows(row_x, grad_pre), contract_rows(row_g, mixed_h)], axis=1)


def on_device(
    tokens, cotangent, route_weight, expert_ids, dense_gate, dense_up, dense_down_t, seed_map
):
    experts = lax.axis_size("expert")
    token_count, feature_count = tokens.shape
    capacity = 3 * token_count * TOP // (2 * experts)
    hidden = dense_gate.shape[1]
    slot_total = experts * capacity
    route_ids = expert_ids[:, 0]
    onehot = (route_ids[:, None] == jnp.arange(experts, dtype=jnp.int32)[None, :]).astype(jnp.int32)
    slot_index = jnp.sum(onehot * (jnp.cumsum(onehot, axis=0) - 1), axis=1)
    target = route_ids * capacity + slot_index
    placer = (target[None, :] == jnp.arange(slot_total, dtype=jnp.int32)[:, None]).astype(
        jnp.bfloat16
    )
    routed = (route_weight[:, None] * cotangent.astype(jnp.float32)).astype(jnp.bfloat16)
    joined_rows = jnp.concatenate([tokens, routed], axis=1)
    placed = jnp.dot(placer, joined_rows, preferred_element_type=jnp.float32).astype(jnp.bfloat16)
    placed = placed.reshape(experts, capacity, 2 * feature_count)
    arrived = lax.all_to_all(placed, "expert", split_axis=0, concat_axis=0, tiled=True).reshape(
        slot_total, 2 * feature_count
    )
    rows_x = arrived[:, :feature_count]
    rows_g = arrived[:, feature_count:]
    owner_slice = lax.dynamic_index_in_dim(seed_map, lax.axis_index("expert"), 0, keepdims=False)
    gate_all, up_all, down_all = (
        lax.all_gather(dense_gate, "expert", axis=1, tiled=True),
        lax.all_gather(dense_up, "expert", axis=1, tiled=True),
        lax.all_gather(dense_down_t, "expert", axis=1, tiled=True),
    )
    first_column = owner_slice * hidden
    local_weights = jnp.concatenate(
        [
            lax.dynamic_slice_in_dim(matrix, first_column, hidden, 1)
            for matrix in (gate_all, up_all, down_all)
        ],
        axis=1,
    )
    piece = lax.all_gather(local_weights, "dp", axis=0, tiled=True)
    cols_x = rows_x
    cols_g = rows_g
    joined_part = jnp.dot(cols_x, piece[:, : 2 * hidden], preferred_element_type=jnp.float32)
    back_part = jnp.dot(cols_g, piece[:, 2 * hidden :], preferred_element_type=jnp.float32)
    mixed_h, grad_pre = activation_grads(joined_part, back_part)
    cols_x = rows_x
    cols_g = rows_g
    summed = lax.psum_scatter(
        weight_terms(cols_x, cols_g, grad_pre, mixed_h), "dp", scatter_dimension=0, tiled=True
    )
    return summed[None]


def solution(mesh):
    return jax.shard_map(
        on_device,
        mesh=mesh,
        in_specs=(
            P(("expert", "dp"), None),
            P(("expert", "dp"), None),
            P(("expert", "dp")),
            P(("expert", "dp"), None),
            P("dp", "expert"),
            P("dp", "expert"),
            P("dp", "expert"),
            P(),
        ),
        out_specs=P("expert", "dp", None),
        check_vma=False,
    )
```

profile of v0, /device:TPU:1, one launch (start us, length us, event | category | flops | bytes accessed | tf_op | source)
XLA Modules:
  0.0 681.6 jit_solution(17387126005003203037)
XLA Ops:
  6.5 0.8 fusion.17
  7.3 0.2 reduce_window_sum.11
  7.5 0.8 select_reduce_fusion
  8.3 0.7 multiply_add_fusion
  9.0 1.3 multiply_convert_fusion
  10.3 0.7 convolution_convert_fusion
  11.0 2.3 reshape.17
  13.2 25.1 %all-to-all-start = ((bf16[32,6,5120]{2,1,0:T(8,128)(2,1)}), bf16[32,6,5120]{2,1,0:T(8,128)(2,1)S(1)}, u32[]{:S(2)}, u32[]{:S(2)}) async-start(bf16[32,6,5120]{2,1,0:T(8,128)(2,1)} %reshape.17), calls=%async_computation | async-start | bytes 5242880 | tf_op jit(solution)/shard_map/all_to_all | solution.py:52
  38.4 0.6 dynamic_slice.13
  39.7 187.5 %all_gather.12 = bf16[80,4096]{1,0:T(8,128)(2,1)S(1)} all-gather(bf16[80,128]{1,0:T(8,128)(2,1)S(1)} %copy-done.2), channel_id=1, replica_groups=mesh['expert'=32,'dp'=32] {'expert'}, dimensions={1}, use_global_device_ids=true | all-gather | bytes 675840 | tf_op jit(solution)/shard_map/all_gather | solution.py:59
  227.2 84.8 %all_gather.13 = bf16[80,4096]{1,0:T(8,128)(2,1)S(1)} all-gather(bf16[80,128]{1,0:T(8,128)(2,1)S(1)} %copy-done.3), channel_id=1, replica_groups=mesh['expert'=32,'dp'=32] {'expert'}, dimensions={1}, use_global_device_ids=true | all-gather | bytes 675840 | tf_op jit(solution)/shard_map/all_gather | solution.py:60
  311.9 81.1 %all_gather.14 = bf16[80,4096]{1,0:T(8,128)(2,1)S(1)} all-gather(bf16[80,128]{1,0:T(8,128)(2,1)S(1)} %copy-done.4), channel_id=1, replica_groups=mesh['expert'=32,'dp'=32] {'expert'}, dimensions={1}, use_global_device_ids=true | all-gather | bytes 675840 | tf_op jit(solution)/shard_map/all_gather | solution.py:61
  393.1 0.6 pad_maximum_fusion.1
  393.8 2.2 reshape.18
  396.0 110.8 %all-gather.2.cloned.1.call-done = bf16[2560,384]{1,0:T(8,128)(2,1)} async-done(((bf16[80,384]{1,0:T(8,128)(2,1)}), bf16[2560,384]{1,0:T(8,128)(2,1)}) %all-gather.2.cloned.1.call-update) | async-done | bytes 1966096 | tf_op jit(solution)/shard_map/all_gather | solution.py:71
  506.7 2.0 fusion
  508.8 0.4 fusion.5
  509.2 1.5 multiply_convert_fusion.3
  510.7 0.6 fusion.9
  511.2 2.1 pad_maximum_fusion
  513.4 5.6 copy.12
  519.0 154.0 %reduce-scatter.4.cloned.1.call-done = f32[80,384]{1,0:T(8,128)} async-done(((f32[2560,384]{1,0:T(8,128)}), f32[80,384]{1,0:T(8,128)}) %reduce-scatter.4.cloned.1.call-update) | async-done | bytes 122896
  672.9 1.0 copy.13
  674.0 0.8 copy.11
  (20 shorter events, 0.2 us)
Async XLA Ops:
  6.5 3.7 copy-start.1
  13.2 25.2 %copy-start.5 = (s32[32]{0:T(128)S(1)}, s32[32]{0:T(128)}, u32[]{:S(2)}) copy-start(s32[32]{0:T(128)} %param.15) | copy-start | bytes 388
  13.2 26.4 %copy-start.2 = (bf16[80,128]{1,0:T(8,128)(2,1)S(1)}, bf16[80,128]{1,0:T(8,128)(2,1)}, u32[]{:S(2)}) copy-start(bf16[80,128]{1,0:T(8,128)(2,1)} %param.12) | copy-start | bytes 61444
  13.2 213.9 %copy-start.3 = (bf16[80,128]{1,0:T(8,128)(2,1)S(1)}, bf16[80,128]{1,0:T(8,128)(2,1)}, u32[]{:S(2)}) copy-start(bf16[80,128]{1,0:T(8,128)(2,1)} %param.13) | copy-start | bytes 61444
  13.2 298.7 %copy-start.4 = (bf16[80,128]{1,0:T(8,128)(2,1)S(1)}, bf16[80,128]{1,0:T(8,128)(2,1)}, u32[]{:S(2)}) copy-start(bf16[80,128]{1,0:T(8,128)(2,1)} %param.14) | copy-start | bytes 61444
  13.2 380.6 %all-to-all-start = ((bf16[32,6,5120]{2,1,0:T(8,128)(2,1)}), bf16[32,6,5120]{2,1,0:T(8,128)(2,1)S(1)}, u32[]{:S(2)}, u32[]{:S(2)}) async-start(bf16[32,6,5120]{2,1,0:T(8,128)(2,1)} %reshape.17), calls=%async_computation | async-start | bytes 5242880 | tf_op jit(solution)/shard_map/all_to_all | solution.py:52
  38.4 468.4 %all-gather.2.cloned.1.call-start = ((), (), s32[]{:S(2)}) async-start(), calls=%async_computation.2 | async-start | bytes 2027520 | tf_op jit(solution)/shard_map/all_gather | solution.py:71
  393.8 279.2 %reduce-scatter.4.cloned.1.call-start = ((), (), s32[]{:S(2)}) async-start(), calls=%async_computation.3 | async-start | bytes 4055040
  396.0 112.8 %copy-start = (bf16[192,5120]{1,0:T(8,128)(2,1)S(1)}, bf16[192,5120]{1,0:T(8,128)(2,1)}, u32[]{:S(2)}) copy-start(bf16[192,5120]{1,0:T(8,128)(2,1)} %reshape.18) | copy-start | bytes 5898244
Sparse Core Ops, SparseCore 0:
  393.9 112.8 all-gather.1
  519.1 153.7 reduce-scatter.3
where the time goes:
time: 683 us; the launch traced here: 682 us
  blocking collectives  353 us (52%)
  waiting for transfers between devices  265 us (39%)
  starting transfers between devices  25.2 us (4%)
  between operations  14.2 us (2%)
  local copies, waits for them, and re-layouts  12.4 us (2%)
    all_gather x1, blocking collectives, on_device(): lax.all_gather(dense_gate, 'expert', axis=1, tiled=True)  187 us
    unnamed x3, waiting for transfers between devices  154 us
    all_gather x1, waiting for transfers between devices, on_device(): piece = lax.all_gather(local_weights, 'dp', axis=0, tiled=True)  111 us
    all_gather x1, blocking collectives, on_device(): lax.all_gather(dense_up, 'expert', axis=1, tiled=True)  84.8 us
    all_gather x1, blocking collectives, on_device(): lax.all_gather(dense_down_t, 'expert', axis=1, tiled=True)  81.1 us
    all_to_all x1, starting transfers between devices, on_device(): lax.all_to_all(placed, 'expert', split_axis=0, concat_axis=0, tiled=True)  25.1 us
  transfers between devices with their start and end apart: 3, of which 2 were waited for; matrix products, arithmetic and copies ran while one was open for 0% of the time, Pallas kernels for 0%

commit v1 on v0

v1 whole, which is shorter than its diff:
```python
import jax
import jax.numpy as jnp
from jax import lax
from jax.experimental import pallas as pl
from jax.experimental.pallas import tpu as pltpu
from jax.sharding import Mesh
from jax.sharding import PartitionSpec as P

EXPERT = ("zh", "zl", "yh")
DP = ("yl", "x", "c")
SIZES = (4, 4, 2, 4, 4, 2)
DISPATCH = ("yl", "zl", "yh")
PIECES = 4
VMEM_LIMIT = 48 * 1024 * 1024


def iota(shape, dim):
    return lax.broadcasted_iota(jnp.int32, shape, dim)


def place_rows(capacity, ids_ref, weight_ref, tokens_ref, cotangent_ref, out_ref):
    count, features = tokens_ref.shape
    half = features // 2
    total = out_ref.shape[0]
    ids_row = ids_ref[...].reshape(1, count)
    weight_row = weight_ref[...].reshape(1, count)
    row, col = iota((count, count), 0), iota((count, count), 1)
    ids_col = jnp.sum(jnp.where(row == col, ids_row, 0), axis=1, keepdims=True)
    weight_col = jnp.sum(jnp.where(row == col, weight_row, 0.0), axis=1, keepdims=True)
    earlier = (ids_col == ids_row) & (row < col)
    slot = jnp.sum(earlier.astype(jnp.int32), axis=0, keepdims=True)
    base = ids_row * (PIECES * capacity) + slot
    routed = (weight_col * cotangent_ref[...].astype(jnp.float32)).astype(jnp.bfloat16)
    target_row = iota((total, 2 * count), 0)

    def placer(piece):
        codes = jnp.concatenate([base + piece * capacity, base + (piece + 1) * capacity], axis=1)
        return jnp.where(target_row == codes, 1.0, 0.0).astype(jnp.bfloat16)

    rows_x = jnp.concatenate([tokens_ref[:, :half], tokens_ref[:, half:]], axis=0)
    rows_g = jnp.concatenate([routed[:, :half], routed[:, half:]], axis=0)
    out = jnp.dot(placer(0), rows_x, preferred_element_type=jnp.float32)
    out += jnp.dot(placer(2), rows_g, preferred_element_type=jnp.float32)
    out_ref[...] = out.astype(jnp.bfloat16)


def pick_slices(index_ref, stack_ref, out_ref, sems):
    copies = [
        pltpu.make_async_copy(stack_ref.at[index_ref[t]], out_ref.at[t], sems.at[t])
        for t in range(out_ref.shape[0])
    ]
    for copy in copies:
        copy.start()
    for copy in copies:
        copy.wait()


def contract_rows(first, second):
    return lax.dot_general(first, second, (((0,), (0,)), ((), ())), preferred_element_type=jnp.float32)


def expert_grads(
    capacity, core_ref, arrived_ref, own_ref, other_ref, mine_ref, theirs_ref, weights, grads, sems
):
    n_x, n_yl = own_ref.shape[:2]
    total, half = arrived_ref.shape
    rows = total // PIECES
    hidden = weights.shape[-1] // 3
    features = 2 * half
    core = core_ref[0]
    copies = []
    for x in range(n_x):
        copies.append(pltpu.make_async_copy(own_ref.at[x], weights.at[:, x, core], sems.at[x]))
        copies.append(
            pltpu.make_async_copy(other_ref.at[x], weights.at[:, x, 1 - core], sems.at[n_x + x])
        )
    for copy in copies:
        copy.start()
    within, column = iota((rows, total), 0), iota((rows, total), 1)
    source = (within * 10923) >> 16
    first = within + source * ((PIECES - 1) * capacity)
    arrived = arrived_ref[...]

    def sorted_rows(piece):
        chosen = jnp.where(column == first + piece * capacity, 1.0, 0.0).astype(jnp.bfloat16)
        return jnp.dot(chosen, arrived, preferred_element_type=jnp.float32).astype(jnp.bfloat16)

    x0, x1, g0, g1 = (sorted_rows(piece) for piece in range(PIECES))
    for copy in copies:
        copy.wait()
    flat = weights[...].reshape(features, 3 * hidden)

    def product(low, high, lanes):
        return jnp.dot(low, flat[:half, lanes], preferred_element_type=jnp.float32) + jnp.dot(
            high, flat[half:, lanes], preferred_element_type=jnp.float32
        )

    joined = product(x0, x1, slice(0, 2 * hidden))
    back = product(g0, g1, slice(2 * hidden, 3 * hidden))
    pre_gate, pre_up = joined[:, :hidden], joined[:, hidden:]
    logistic = jax.nn.sigmoid(pre_gate)
    gated = pre_gate * logistic
    slope = logistic * (1.0 + pre_gate * (1.0 - logistic))
    mixed = (gated * pre_up).astype(jnp.bfloat16)
    grad_pre = jnp.concatenate([back * pre_up * slope, back * gated], axis=1).astype(jnp.bfloat16)
    n_half = n_yl // 2
    blocks = (n_half, n_x, 2, weights.shape[3])
    for part, (rows_x, rows_g) in enumerate(((x0, g0), (x1, g1))):
        at = slice(part * n_half, (part + 1) * n_half)
        grads[at, :, :, :, : 2 * hidden] = contract_rows(rows_x, grad_pre).reshape(
            blocks + (2 * hidden,)
        )
        grads[at, :, :, :, 2 * hidden :] = contract_rows(rows_g, mixed).reshape(blocks + (hidden,))
    for x in range(n_x):
        mine_ref[x] = grads[:, x, core]
        theirs_ref[x] = grads[:, x, 1 - core].astype(jnp.bfloat16)


def on_device(
    tokens, cotangent, route_weight, expert_ids, dense_gate, dense_up, dense_down_t, seed_map
):
    n_zh, n_zl, n_yh, n_yl, n_x, n_c = SIZES
    experts = n_zh * n_zl * n_yh
    count, features = tokens.shape
    capacity = 3 * count // (2 * experts)
    half = features // 2
    block, hidden = dense_gate.shape
    width = 3 * hidden
    chunk = PIECES * capacity
    vmem = pl.BlockSpec(memory_space=pltpu.VMEM)
    smem = pl.BlockSpec(memory_space=pltpu.SMEM)
    anywhere = pl.BlockSpec(memory_space=pl.ANY)
    params = pltpu.CompilerParams(vmem_limit_bytes=VMEM_LIMIT)
    bf16 = jnp.bfloat16

    placed = pl.pallas_call(
        lambda *refs: place_rows(capacity, *refs),
        out_shape=jax.ShapeDtypeStruct((experts * chunk, half), bf16),
        in_specs=[vmem] * 4,
        out_specs=vmem,
        compiler_params=params,
        name="place_rows",
    )(expert_ids[:, 0], route_weight, tokens, cotangent)
    arrived = lax.all_to_all(
        placed.reshape(experts, chunk, half), DISPATCH, split_axis=0, concat_axis=0, tiled=True
    ).reshape(experts * chunk, half)

    zl, zh = lax.axis_index("zl"), lax.axis_index("zh")
    core = lax.axis_index("c")
    own = jnp.concatenate([dense_gate, dense_up, dense_down_t], axis=1)
    slices = lax.all_gather(own, ("zh", "zl"), axis=0, tiled=False)
    seeds = lax.dynamic_index_in_dim(seed_map.reshape(n_zh, n_zl, n_yh), zl, 1, keepdims=False).T
    offered = pl.pallas_call(
        pick_slices,
        out_shape=jax.ShapeDtypeStruct((n_yh * n_yl, block, width), bf16),
        in_specs=[smem, anywhere],
        out_specs=anywhere,
        scratch_shapes=[pltpu.SemaphoreType.DMA((n_yh * n_yl,))],
        compiler_params=params,
        name="pick_slices",
    )((seeds // n_yh).reshape(-1), slices)
    sent = lax.all_to_all(offered, ("yh", "yl"), split_axis=0, concat_axis=0, tiled=True)
    my_seed = seeds[lax.axis_index("yh"), lax.axis_index("yl")]
    seeded = lax.dynamic_slice_in_dim(sent, (my_seed % n_yh) * n_yl, n_yl, 0)
    own_rows = lax.all_gather(seeded, "x", axis=0, tiled=False)
    swap = [(i, 1 - i) for i in range(n_c)]
    other_rows = lax.ppermute(own_rows, "c", swap)

    half_shape = (n_x, n_yl, block, width)
    mine, theirs = pl.pallas_call(
        lambda *refs: expert_grads(capacity, *refs),
        out_shape=[
            jax.ShapeDtypeStruct(half_shape, jnp.float32),
            jax.ShapeDtypeStruct(half_shape, bf16),
        ],
        in_specs=[smem, vmem, anywhere, anywhere],
        out_specs=[vmem, vmem],
        scratch_shapes=[
            pltpu.VMEM((n_yl, n_x, n_c, block, width), bf16),
            pltpu.VMEM((n_yl, n_x, n_c, block, width), jnp.float32),
            pltpu.SemaphoreType.DMA((2 * n_x,)),
        ],
        compiler_params=params,
        name="expert_grads",
    )(core.reshape(1), arrived, own_rows, other_rows)
    pair = (mine + lax.ppermute(theirs, "c", swap).astype(jnp.float32)).astype(bf16)
    by_x = lax.all_to_all(pair, "x", split_axis=0, concat_axis=0, tiled=True)
    row_sums = jnp.sum(by_x.astype(jnp.float32), axis=0).astype(bf16)
    total = None
    for step in range(n_yl):
        part = lax.dynamic_index_in_dim(row_sums, (zh + step) % n_yl, 0, keepdims=False)
        moves = [
            (a * n_yl + b, b * n_yl + (a + step) % n_yl) for a in range(n_zh) for b in range(n_yl)
        ]
        got = lax.ppermute(part, ("zh", "yl"), moves).astype(jnp.float32)
        total = got if total is None else total + got
    return total[None]


def solution(mesh):
    fine = Mesh(mesh.devices.reshape(SIZES), EXPERT + DP)
    rows = P(EXPERT + DP, None)
    dense = P(DP, EXPERT)
    return jax.shard_map(
        on_device,
        mesh=fine,
        in_specs=(rows, rows, P(EXPERT + DP), rows, dense, dense, dense, P()),
        out_specs=P(EXPERT, DP, None),
        check_vma=False,
    )
```

time: 683 us -> 192 us (0.28)
  blocking collectives: 353 us -> 53.1 us
  waiting for transfers between devices: 265 us -> 61.4 us
  starting transfers between devices: 25.2 us -> 60.2 us
  between operations: 14.2 us -> 2.14 us
  local copies, waits for them, and re-layouts: 12.4 us -> 1.72 us
  Pallas kernels: 0 us -> 9.73 us
    all_gather x3 -> x2, blocking collectives: 353 us -> 53.1 us  [the longest x1 41.9 us: on_device(): slices = lax.all_gather(own, ('zh', 'zl'), axis=0, tiled=False)]
    unnamed x3 -> x0, waiting for transfers between devices: 154 us -> none
    all_gather x1 -> x0, waiting for transfers between devices: 111 us -> none  [on_device(): piece = lax.all_gather(local_weights, 'dp', axis=0, tiled=True)]
    ppermute x0 -> x6, starting transfers between devices: none -> 44.6 us  [the longest x4 23.2 us: on_device(): got = lax.ppermute(part, ('zh', 'yl'), moves).astype(jnp.float32)]
    all_to_all x1 -> x3, waiting for transfers between devices: 0.01 us -> 37.4 us  [the longest x1 14.5 us: on_device(): lax.all_to_all(placed.reshape(experts, chunk, half), DISPATCH, split_axis...]
    ppermute x0 -> x6, waiting for transfers between devices: none -> 24 us  [the longest x4 19.6 us: on_device(): got = lax.ppermute(part, ('zh', 'yl'), moves).astype(jnp.float32)]
    pallas_call x0 -> x3, Pallas kernels: none -> 9.73 us  [the longest x1 5.68 us: on_device(): pl.pallas_call(lambda *refs: expert_grads(capacity, *refs), out_shape=[ja...]
    all_to_all x1 -> x3, starting transfers between devices: 25.1 us -> 15.6 us  [the longest x1 6.83 us: on_device(): lax.all_to_all(offered, ('yh', 'yl'), split_axis=0, concat_axis=0, tiled=...]
  transfers between devices with their start and end apart: 3 -> 9, of which waited for: 2 -> 7; matrix products, arithmetic and copies ran while one was open for 0% -> 0% of each run, Pallas kernels for 0% -> 1%
where the time goes in v1:
time: 192 us; the launch traced here: 191 us
  waiting for transfers between devices  61.4 us (32%)
  starting transfers between devices  60.2 us (31%)
  blocking collectives  53.1 us (28%)
  Pallas kernels  9.73 us (5%)
  other arithmetic  2.86 us (1%)
  between operations  2.14 us (1%)
    all_gather x1, blocking collectives, on_device(): slices = lax.all_gather(own, ('zh', 'zl'), axis=0, tiled=False)  41.9 us
    ppermute x4, starting transfers between devices, on_device(): got = lax.ppermute(part, ('zh', 'yl'), moves).astype(jnp.float32)  23.2 us
    ppermute x4, waiting for transfers between devices, on_device(): got = lax.ppermute(part, ('zh', 'yl'), moves).astype(jnp.float32)  19.6 us
    all_to_all x1, waiting for transfers between devices, on_device(): lax.all_to_all(placed.reshape(experts, chunk, half), DISPATCH, split_axis...  14.5 us
    all_to_all x1, waiting for transfers between devices, on_device(): by_x = lax.all_to_all(pair, 'x', split_axis=0, concat_axis=0, tiled=True)  13.8 us
    ppermute x1, starting transfers between devices, on_device(): other_rows = lax.ppermute(own_rows, 'c', swap)  13.8 us
    all_gather x1, blocking collectives, on_device(): own_rows = lax.all_gather(seeded, 'x', axis=0, tiled=False)  11.2 us
    all_to_all x1, waiting for transfers between devices, on_device(): lax.all_to_all(offered, ('yh', 'yl'), split_axis=0, concat_axis=0, tiled=...  9.11 us
  transfers between devices with their start and end apart: 9, of which 7 were waited for; matrix products, arithmetic and copies ran while one was open for 0% of the time, Pallas kernels for 1%

profile of v1, /device:TPU:1, one launch (start us, length us, event | category | flops | bytes accessed | tf_op | source)
XLA Modules:
  0.0 191.1 jit_solution(6725453404967336592)
XLA Ops:
  0.0 0.8 reshape.22
  1.1 0.8 pad_maximum_fusion
  1.9 41.9 %all-gather = bf16[1280,384]{1,0:T(8,128)(2,1)S(1)} all-gather(bf16[80,384]{1,0:T(8,128)(2,1)S(1)} %pad_maximum_fusion), channel_id=2, replica_groups=mesh['zh'=4,'zl'=4,'yh'=2,'yl'=4,'x'=4,'c'=2] {'zh','zl'}, dimensions={0}, use_global_device_ids=true | all-gather | bytes 1044480 | tf_op jit(solution)/shard_map/all_gather | solution.py:151
  43.8 1.4 pick_slices.1
  45.2 6.8 %all-to-all-start.1 = ((bf16[8,80,384]{2,1,0:T(8,128)(2,1)}), bf16[8,80,384]{2,1,0:T(8,128)(2,1)S(1)}, u32[]{:S(2)}, u32[]{:S(2)}) async-start(bf16[8,80,384]{2,1,0:T(8,128)(2,1)} %pick_slices.1), calls=%async_computation.1 | async-start | bytes 983040 | tf_op jit(solution)/shard_map/all_to_all | solution.py:162
  52.1 2.6 %place_rows.1 = bf16[768,1280]{1,0:T(8,128)(2,1)} custom-call(s32[128]{0:T(128)S(1)} %bitcast.30, f32[128]{0:T(128)S(1)} %copy-done.3, bf16[128,2560]{1,0:T(8,128)(2,1)S(1)} %copy-done, bf16[128,2560]{1,0:T(8,128)(2,1)S(1)} %copy-done.1), custom_call_target="tpu_custom_call" | custom-call | tf_op jit(solution)/shard_map/place_rows/pallas_call | solution.py:136
  54.7 9.1 %all-to-all-done.1 = bf16[8,80,384]{2,1,0:T(8,128)(2,1)S(1)} async-done(((bf16[8,80,384]{2,1,0:T(8,128)(2,1)}), bf16[8,80,384]{2,1,0:T(8,128)(2,1)S(1)}, u32[]{:S(2)}, u32[]{:S(2)}) %all-to-all-start.1) | async-done | bytes 491552 | tf_op jit(solution)/shard_map/all_to_all | solution.py:162
  63.8 4.7 %all-to-all-start = ((bf16[32,24,1280]{2,1,0:T(8,128)(2,1)}), bf16[32,24,1280]{2,1,0:T(8,128)(2,1)}, u32[]{:S(2)}, u32[]{:S(2)}) async-start(bf16[32,24,1280]{2,1,0:T(8,128)(2,1)} %bitcast.2), calls=%async_computation | async-start | bytes 3932160 | tf_op jit(solution)/shard_map/all_to_all | solution.py:144
  71.2 11.2 %all-gather.1 = bf16[16,80,384]{2,1,0:T(8,128)(2,1)S(1)} all-gather(bf16[4,80,384]{2,1,0:T(8,128)(2,1)S(1)} %constant_dynamic-slice_fusion), channel_id=3, replica_groups=mesh['zh'=4,'zl'=4,'yh'=2,'yl'=4,'x'=4,'c'=2] {'x'}, dimensions={0}, use_global_device_ids=true | all-gather | bytes 1228800 | tf_op jit(solution)/shard_map/all_gather | solution.py:165
  82.3 13.8 %collective-permute-start = (bf16[4,4,80,384]{3,2,1,0:T(8,128)(2,1)S(1)}, bf16[4,4,80,384]{3,2,1,0:T(8,128)(2,1)S(1)}, u32[]{:S(2)}, u32[]{:S(2)}) collective-permute-start(bf16[4,4,80,384]{3,2,1,0:T(8,128)(2,1)S(1)} %bitcast.28), channel_id=1, source_target_pairs={{0,1},{1,0},{2,3},{3,2},{4,5},{5,4},{6,7},{7,6},{8,9},{9,8},{10,11... | collective-permute-start | bytes 2949128 | tf_op jit(solution)/shard_map/ppermute | solution.py:167
  96.2 2.2 %collective-permute-done.refs_3_ = bf16[4,4,80,384]{3,2,1,0:T(8,128)(2,1)S(1)} collective-permute-done((bf16[4,4,80,384]{3,2,1,0:T(8,128)(2,1)S(1)}, bf16[4,4,80,384]{3,2,1,0:T(8,128)(2,1)S(1)}, u32[]{:S(2)}, u32[]{:S(2)}) %collective-permute-start) | collective-permute-done | bytes 983072 | tf_op jit(solution)/shard_map/ppermute | solution.py:167
  98.3 14.5 %all-to-all-done = bf16[32,24,1280]{2,1,0:T(8,128)(2,1)} async-done(((bf16[32,24,1280]{2,1,0:T(8,128)(2,1)}), bf16[32,24,1280]{2,1,0:T(8,128)(2,1)}, u32[]{:S(2)}, u32[]{:S(2)}) %all-to-all-start) | async-done | bytes 1966112 | tf_op jit(solution)/shard_map/all_to_all | solution.py:144
  112.8 5.7 %expert_grads.1 = (f32[4,4,80,384]{3,2,1,0:T(8,128)S(1)}, bf16[4,4,80,384]{3,2,1,0:T(8,128)(2,1)S(1)}) custom-call(s32[1]{0:T(128)} %bitcast.refs_0_, bf16[768,1280]{1,0:T(8,128)(2,1)} %bitcast.3.refs_1_, bf16[4,4,80,384]{3,2,1,0:T(8,128)(2,1)S(1)} %bitcast.29, bf16[4,4,80,384]{3,2,1,0:T(8,128)(2,1)S(1)} %collective-permute-done.refs_3_), custom_call_target="tpu_custom_call" | custom-call | tf_op jit(solution)/shard_map/expert_grads/pallas_call | solution.py:170
  118.5 7.7 %collective-permute-start.1 = (bf16[4,4,80,384]{3,2,1,0:T(8,128)(2,1)S(1)}, bf16[4,4,80,384]{3,2,1,0:T(8,128)(2,1)S(1)}, u32[]{:S(2)}, u32[]{:S(2)}) collective-permute-start(bf16[4,4,80,384]{3,2,1,0:T(8,128)(2,1)S(1)} %get-tuple-element.8), channel_id=1, source_target_pairs={{0,1},{1,0},{2,3},{3,2},{4,5},{5,4},{6,7},{7,6},{8,9},{9,8},{10,11... | collective-permute-start | bytes 2949128 | tf_op jit(solution)/shard_map/ppermute | solution.py:186
  126.2 2.2 %collective-permute-done.1 = bf16[4,4,80,384]{3,2,1,0:T(8,128)(2,1)S(1)} collective-permute-done((bf16[4,4,80,384]{3,2,1,0:T(8,128)(2,1)S(1)}, bf16[4,4,80,384]{3,2,1,0:T(8,128)(2,1)S(1)}, u32[]{:S(2)}, u32[]{:S(2)}) %collective-permute-start.1) | collective-permute-done | bytes 983072 | tf_op jit(solution)/shard_map/ppermute | solution.py:186
  128.3 1.2 add_convert_fusion
  129.5 4.0 %all-to-all-start.2 = ((bf16[4,4,80,384]{3,2,1,0:T(8,128)(2,1)}), bf16[4,4,80,384]{3,2,1,0:T(8,128)(2,1)S(1)}, u32[]{:S(2)}, u32[]{:S(2)}) async-start(bf16[4,4,80,384]{3,2,1,0:T(8,128)(2,1)} %add_convert_fusion), calls=%async_computation.2 | async-start | bytes 1966080 | tf_op jit(solution)/shard_map/all_to_all | solution.py:187
  133.5 13.8 %all-to-all-done.2 = bf16[4,4,80,384]{3,2,1,0:T(8,128)(2,1)S(1)} async-done(((bf16[4,4,80,384]{3,2,1,0:T(8,128)(2,1)}), bf16[4,4,80,384]{3,2,1,0:T(8,128)(2,1)S(1)}, u32[]{:S(2)}, u32[]{:S(2)}) %all-to-all-start.2) | async-done | bytes 983072 | tf_op jit(solution)/shard_map/all_to_all | solution.py:187
  147.6 0.7 collective-permute-start.2
  148.3 8.8 %collective-permute-start.3 = (bf16[80,384]{1,0:T(8,128)(2,1)S(1)}, bf16[80,384]{1,0:T(8,128)(2,1)S(1)}, u32[]{:S(2)}, u32[]{:S(2)}) collective-permute-start(bf16[80,384]{1,0:T(8,128)(2,1)S(1)} %get-tuple-element.12), channel_id=1, source_target_pairs={{0,8},{8,264},{16,520},{24,776},{256,16},{264,272},{272,528},{280,... | collective-permute-start | bytes 184328 | tf_op jit(solution)/shard_map/ppermute | solution.py:195
  157.1 6.4 %collective-permute-start.4 = (bf16[80,384]{1,0:T(8,128)(2,1)S(1)}, bf16[80,384]{1,0:T(8,128)(2,1)S(1)}, u32[]{:S(2)}, u32[]{:S(2)}) collective-permute-start(bf16[80,384]{1,0:T(8,128)(2,1)S(1)} %get-tuple-element.11), channel_id=1, source_target_pairs={{0,16},{8,272},{16,528},{24,784},{256,24},{264,280},{272,536},{280... | collective-permute-start | bytes 184328 | tf_op jit(solution)/shard_map/ppermute | solution.py:195
  163.5 7.3 %collective-permute-start.5 = (bf16[80,384]{1,0:T(8,128)(2,1)S(1)}, bf16[80,384]{1,0:T(8,128)(2,1)S(1)}, u32[]{:S(2)}, u32[]{:S(2)}) collective-permute-start(bf16[80,384]{1,0:T(8,128)(2,1)S(1)} %get-tuple-element.10), channel_id=1, source_target_pairs={{0,24},{8,280},{16,536},{24,792},{256,0},{264,256},{272,512},{280,... | collective-permute-start | bytes 184328 | tf_op jit(solution)/shard_map/ppermute | solution.py:195
  171.2 19.2 %collective-permute-done.5 = bf16[80,384]{1,0:T(8,128)(2,1)S(1)} collective-permute-done((bf16[80,384]{1,0:T(8,128)(2,1)S(1)}, bf16[80,384]{1,0:T(8,128)(2,1)S(1)}, u32[]{:S(2)}, u32[]{:S(2)}) %collective-permute-start.5) | collective-permute-done | bytes 61472 | tf_op jit(solution)/shard_map/ppermute | solution.py:195
  190.5 0.7 add_bitcast_fusion
  (19 shorter events, 1.5 us)
Async XLA Ops:
  0.0 52.0 %copy-start.2 = (s32[128,1]{0,1:T(1,128)S(1)}, s32[128,1]{0,1:T(1,128)}, u32[]{:S(2)}) copy-start(s32[128,1]{0,1:T(1,128)} %param.11) | copy-start | bytes 1540
  0.0 52.0 %copy-start.3 = (f32[128]{0:T(128)S(1)}, f32[128]{0:T(128)}, u32[]{:S(2)}) copy-start(f32[128]{0:T(128)} %refs_1_.1) | copy-start | bytes 1540
  0.0 52.0 %copy-start = (bf16[128,2560]{1,0:T(8,128)(2,1)S(1)}, bf16[128,2560]{1,0:T(8,128)(2,1)}, u32[]{:S(2)}) copy-start(bf16[128,2560]{1,0:T(8,128)(2,1)} %refs_2_.1) | copy-start | bytes 1966084
  0.0 52.0 %copy-start.1 = (bf16[128,2560]{1,0:T(8,128)(2,1)S(1)}, bf16[128,2560]{1,0:T(8,128)(2,1)}, u32[]{:S(2)}) copy-start(bf16[128,2560]{1,0:T(8,128)(2,1)} %refs_3_.1) | copy-start | bytes 1966084
  45.2 18.6 %all-to-all-start.1 = ((bf16[8,80,384]{2,1,0:T(8,128)(2,1)}), bf16[8,80,384]{2,1,0:T(8,128)(2,1)S(1)}, u32[]{:S(2)}, u32[]{:S(2)}) async-start(bf16[8,80,384]{2,1,0:T(8,128)(2,1)} %pick_slices.1), calls=%async_computation.1 | async-start | bytes 983040 | tf_op jit(solution)/shard_map/all_to_all | solution.py:162
  63.8 49.0 %all-to-all-start = ((bf16[32,24,1280]{2,1,0:T(8,128)(2,1)}), bf16[32,24,1280]{2,1,0:T(8,128)(2,1)}, u32[]{:S(2)}, u32[]{:S(2)}) async-start(bf16[32,24,1280]{2,1,0:T(8,128)(2,1)} %bitcast.2), calls=%async_computation | async-start | bytes 3932160 | tf_op jit(solution)/shard_map/all_to_all | solution.py:144
  82.3 16.0 %collective-permute-start = (bf16[4,4,80,384]{3,2,1,0:T(8,128)(2,1)S(1)}, bf16[4,4,80,384]{3,2,1,0:T(8,128)(2,1)S(1)}, u32[]{:S(2)}, u32[]{:S(2)}) collective-permute-start(bf16[4,4,80,384]{3,2,1,0:T(8,128)(2,1)S(1)} %bitcast.28), channel_id=1, source_target_pairs={{0,1},{1,0},{2,3},{3,2},{4,5},{5,4},{6,7},{7,6},{8,9},{9,8},{10,11... | collective-permute-start | bytes 2949128 | tf_op jit(solution)/shard_map/ppermute | solution.py:167
  118.5 9.8 %collective-permute-start.1 = (bf16[4,4,80,384]{3,2,1,0:T(8,128)(2,1)S(1)}, bf16[4,4,80,384]{3,2,1,0:T(8,128)(2,1)S(1)}, u32[]{:S(2)}, u32[]{:S(2)}) collective-permute-start(bf16[4,4,80,384]{3,2,1,0:T(8,128)(2,1)S(1)} %get-tuple-element.8), channel_id=1, source_target_pairs={{0,1},{1,0},{2,3},{3,2},{4,5},{5,4},{6,7},{7,6},{8,9},{9,8},{10,11... | collective-permute-start | bytes 2949128 | tf_op jit(solution)/shard_map/ppermute | solution.py:186
  129.5 17.8 %all-to-all-start.2 = ((bf16[4,4,80,384]{3,2,1,0:T(8,128)(2,1)}), bf16[4,4,80,384]{3,2,1,0:T(8,128)(2,1)S(1)}, u32[]{:S(2)}, u32[]{:S(2)}) async-start(bf16[4,4,80,384]{3,2,1,0:T(8,128)(2,1)} %add_convert_fusion), calls=%async_computation.2 | async-start | bytes 1966080 | tf_op jit(solution)/shard_map/all_to_all | solution.py:187
  147.6 23.2 %collective-permute-start.2 = (bf16[80,384]{1,0:T(8,128)(2,1)S(1)}, bf16[80,384]{1,0:T(8,128)(2,1)S(1)}, u32[]{:S(2)}, u32[]{:S(2)}) collective-permute-start(bf16[80,384]{1,0:T(8,128)(2,1)S(1)} %get-tuple-element.9), channel_id=1, source_target_pairs={{0,0},{8,256},{16,512},{24,768},{256,8},{264,264},{272,520},{280,7... | collective-permute-start | bytes 184328 | tf_op jit(solution)/shard_map/ppermute | solution.py:195
  148.3 22.5 %collective-permute-start.3 = (bf16[80,384]{1,0:T(8,128)(2,1)S(1)}, bf16[80,384]{1,0:T(8,128)(2,1)S(1)}, u32[]{:S(2)}, u32[]{:S(2)}) collective-permute-start(bf16[80,384]{1,0:T(8,128)(2,1)S(1)} %get-tuple-element.12), channel_id=1, source_target_pairs={{0,8},{8,264},{16,520},{24,776},{256,16},{264,272},{272,528},{280,... | collective-permute-start | bytes 184328 | tf_op jit(solution)/shard_map/ppermute | solution.py:195
  157.1 14.1 %collective-permute-start.4 = (bf16[80,384]{1,0:T(8,128)(2,1)S(1)}, bf16[80,384]{1,0:T(8,128)(2,1)S(1)}, u32[]{:S(2)}, u32[]{:S(2)}) collective-permute-start(bf16[80,384]{1,0:T(8,128)(2,1)S(1)} %get-tuple-element.11), channel_id=1, source_target_pairs={{0,16},{8,272},{16,528},{24,784},{256,24},{264,280},{272,536},{280... | collective-permute-start | bytes 184328 | tf_op jit(solution)/shard_map/ppermute | solution.py:195
  163.5 27.0 %collective-permute-start.5 = (bf16[80,384]{1,0:T(8,128)(2,1)S(1)}, bf16[80,384]{1,0:T(8,128)(2,1)S(1)}, u32[]{:S(2)}, u32[]{:S(2)}) collective-permute-start(bf16[80,384]{1,0:T(8,128)(2,1)S(1)} %get-tuple-element.10), channel_id=1, source_target_pairs={{0,24},{8,280},{16,536},{24,792},{256,0},{264,256},{272,512},{280,... | collective-permute-start | bytes 184328 | tf_op jit(solution)/shard_map/ppermute | solution.py:195

commit v2 on v1

--- a/solution.py
+++ b/solution.py
@@ -44,11 +44,16 @@
     out_ref[...] = out.astype(jnp.bfloat16)
 
 
-def pick_slices(index_ref, stack_ref, out_ref, sems):
-    copies = [
-        pltpu.make_async_copy(stack_ref.at[index_ref[t]], out_ref.at[t], sems.at[t])
-        for t in range(out_ref.shape[0])
-    ]
+def pick_slices(zl_ref, seeds_ref, stack_ref, out_ref, sems):
+    _, n_zl, n_yh, n_yl, _, _ = SIZES
+    copies = []
+    for yh in range(n_yh):
+        for yl in range(n_yl):
+            seed = seeds_ref[(yl * n_zl + zl_ref[0]) * n_yh + yh]
+            to = yh * n_yl + yl
+            copies.append(
+                pltpu.make_async_copy(stack_ref.at[seed // n_yh], out_ref.at[to], sems.at[to])
+            )
     for copy in copies:
         copy.start()
     for copy in copies:
@@ -145,22 +150,20 @@
         placed.reshape(experts, chunk, half), DISPATCH, split_axis=0, concat_axis=0, tiled=True
     ).reshape(experts * chunk, half)
 
-    zl, zh = lax.axis_index("zl"), lax.axis_index("zh")
-    core = lax.axis_index("c")
+    zl, core = lax.axis_index("zl"), lax.axis_index("c")
     own = jnp.concatenate([dense_gate, dense_up, dense_down_t], axis=1)
     slices = lax.all_gather(own, ("zh", "zl"), axis=0, tiled=False)
-    seeds = lax.dynamic_index_in_dim(seed_map.reshape(n_zh, n_zl, n_yh), zl, 1, keepdims=False).T
     offered = pl.pallas_call(
         pick_slices,
         out_shape=jax.ShapeDtypeStruct((n_yh * n_yl, block, width), bf16),
-        in_specs=[smem, anywhere],
+        in_specs=[smem, smem, anywhere],
         out_specs=anywhere,
         scratch_shapes=[pltpu.SemaphoreType.DMA((n_yh * n_yl,))],
         compiler_params=params,
         name="pick_slices",
-    )((seeds // n_yh).reshape(-1), slices)
+    )(zl.reshape(1), seed_map, slices)
     sent = lax.all_to_all(offered, ("yh", "yl"), split_axis=0, concat_axis=0, tiled=True)
-    my_seed = seeds[lax.axis_index("yh"), lax.axis_index("yl")]
+    my_seed = seed_map[lax.axis_index(DISPATCH)]
     seeded = lax.dynamic_slice_in_dim(sent, (my_seed % n_yh) * n_yl, n_yl, 0)
     own_rows = lax.all_gather(seeded, "x", axis=0, tiled=False)
     swap = [(i, 1 - i) for i in range(n_c)]
@@ -186,14 +189,9 @@
     pair = (mine + lax.ppermute(theirs, "c", swap).astype(jnp.float32)).astype(bf16)
     by_x = lax.all_to_all(pair, "x", split_axis=0, concat_axis=0, tiled=True)
     row_sums = jnp.sum(by_x.astype(jnp.float32), axis=0).astype(bf16)
-    total = None
-    for step in range(n_yl):
-        part = lax.dynamic_index_in_dim(row_sums, (zh + step) % n_yl, 0, keepdims=False)
-        moves = [
-            (a * n_yl + b, b * n_yl + (a + step) % n_yl) for a in range(n_zh) for b in range(n_yl)
-        ]
-        got = lax.ppermute(part, ("zh", "yl"), moves).astype(jnp.float32)
-        total = got if total is None else total + got
+    by_home = lax.all_to_all(row_sums, "yl", split_axis=0, concat_axis=0, tiled=True)
+    by_group = lax.all_to_all(by_home, "zh", split_axis=0, concat_axis=0, tiled=True)
+    total = jnp.sum(by_group.astype(jnp.float32), axis=0)
     return total[None]
 
 

time: 192 us -> 184 us (0.958); the launches traced: 191 us -> 181 us
  blocking collectives: 53.1 us -> 104 us
  waiting for transfers between devices: 61.4 us -> 28.2 us
  starting transfers between devices: 60.2 us -> 33.1 us
    all_to_all x0 -> x3, blocking collectives: none -> 51.2 us  [the longest x1 21.3 us: on_device(): lax.all_to_all(by_home, 'zh', split_axis=0, concat_axis=0, tiled=True)]
    ppermute x4 -> x0, starting transfers between devices: 23.2 us -> none  [on_device(): got = lax.ppermute(part, ('zh', 'yl'), moves).astype(jnp.float32)]
    ppermute x4 -> x0, waiting for transfers between devices: 19.6 us -> none  [on_device(): got = lax.ppermute(part, ('zh', 'yl'), moves).astype(jnp.float32)]
    all_to_all x1 -> x0, waiting for transfers between devices: 13.8 us -> none  [on_device(): by_x = lax.all_to_all(pair, 'x', split_axis=0, concat_axis=0, tiled=True)]
    all_to_all x1 -> x0, starting transfers between devices: 4.01 us -> none  [on_device(): by_x = lax.all_to_all(pair, 'x', split_axis=0, concat_axis=0, tiled=True)]
  transfers between devices with their start and end apart: 9 -> 4, of which waited for: 7 -> 4; matrix products, arithmetic and copies ran while one was open for 0% -> 0% of each run, Pallas kernels for 1% -> 1%
where the time goes in v2:
time: 184 us; the launch traced here: 181 us
  blocking collectives  104 us (57%)
  starting transfers between devices  33.1 us (18%)
  waiting for transfers between devices  28.2 us (15%)
  Pallas kernels  9.73 us (5%)
  between operations  2.07 us (1%)
  other arithmetic  2 us (1%)
    all_gather x1, blocking collectives, on_device(): slices = lax.all_gather(own, ('zh', 'zl'), axis=0, tiled=False)  41.9 us
    all_to_all x1, blocking collectives, on_device(): lax.all_to_all(by_home, 'zh', split_axis=0, concat_axis=0, tiled=True)  21.3 us
    all_to_all x1, blocking collectives, on_device(): by_x = lax.all_to_all(pair, 'x', split_axis=0, concat_axis=0, tiled=True)  17.6 us
    all_to_all x1, waiting for transfers between devices, on_device(): lax.all_to_all(placed.reshape(experts, chunk, half), DISPATCH, split_axis...  14.7 us
    ppermute x1, starting transfers between devices, on_device(): other_rows = lax.ppermute(own_rows, 'c', swap)  13.8 us
    all_to_all x1, blocking collectives, on_device(): lax.all_to_all(row_sums, 'yl', split_axis=0, concat_axis=0, tiled=True)  12.3 us
    all_gather x1, blocking collectives, on_device(): own_rows = lax.all_gather(seeded, 'x', axis=0, tiled=False)  11.2 us
    all_to_all x1, waiting for transfers between devices, on_device(): lax.all_to_all(offered, ('yh', 'yl'), split_axis=0, concat_axis=0, tiled=...  9.11 us
  transfers between devices with their start and end apart: 4, of which 4 were waited for; matrix products, arithmetic and copies ran while one was open for 0% of the time, Pallas kernels for 1%

profile of v2, /device:TPU:1, one launch (start us, length us, event | category | flops | bytes accessed | tf_op | source)
XLA Modules:
  0.0 180.7 jit_solution(10144905717332926415)
XLA Ops:
  0.0 0.9 pad_maximum_fusion
  0.9 41.9 %all-gather = bf16[1280,384]{1,0:T(8,128)(2,1)S(1)} all-gather(bf16[80,384]{1,0:T(8,128)(2,1)S(1)} %pad_maximum_fusion), channel_id=2, replica_groups=mesh['zh'=4,'zl'=4,'yh'=2,'yl'=4,'x'=4,'c'=2] {'zh','zl'}, dimensions={0}, use_global_device_ids=true | all-gather | bytes 1044480 | tf_op jit(solution)/shard_map/all_gather | solution.py:155
  42.8 0.7 copy-done.2
  43.5 1.4 pick_slices.1
  44.9 6.8 %all-to-all-start.1 = ((bf16[8,80,384]{2,1,0:T(8,128)(2,1)}), bf16[8,80,384]{2,1,0:T(8,128)(2,1)S(1)}, u32[]{:S(2)}, u32[]{:S(2)}) async-start(bf16[8,80,384]{2,1,0:T(8,128)(2,1)} %pick_slices.1), calls=%async_computation.1 | async-start | bytes 983040 | tf_op jit(solution)/shard_map/all_to_all | solution.py:165
  51.7 0.0 copy-done.1
  51.7 0.0 copy-done
  51.7 2.6 %place_rows.1 = bf16[768,1280]{1,0:T(8,128)(2,1)} custom-call(s32[128]{0:T(128)S(1)} %bitcast.12, f32[128]{0:T(128)S(1)} %copy-done.5, bf16[128,2560]{1,0:T(8,128)(2,1)S(1)} %copy-done, bf16[128,2560]{1,0:T(8,128)(2,1)S(1)} %copy-done.1), custom_call_target="tpu_custom_call" | custom-call | tf_op jit(solution)/shard_map/place_rows/pallas_call | solution.py:141
  54.4 9.1 %all-to-all-done.1 = bf16[8,80,384]{2,1,0:T(8,128)(2,1)S(1)} async-done(((bf16[8,80,384]{2,1,0:T(8,128)(2,1)}), bf16[8,80,384]{2,1,0:T(8,128)(2,1)S(1)}, u32[]{:S(2)}, u32[]{:S(2)}) %all-to-all-start.1) | async-done | bytes 491552 | tf_op jit(solution)/shard_map/all_to_all | solution.py:165
  63.5 4.9 %all-to-all-start = ((bf16[32,24,1280]{2,1,0:T(8,128)(2,1)}), bf16[32,24,1280]{2,1,0:T(8,128)(2,1)}, u32[]{:S(2)}, u32[]{:S(2)}) async-start(bf16[32,24,1280]{2,1,0:T(8,128)(2,1)} %bitcast.2), calls=%async_computation | async-start | bytes 3932160 | tf_op jit(solution)/shard_map/all_to_all | solution.py:149
  68.4 0.6 dynamic_slice.6
  71.0 11.2 %all-gather.1 = bf16[16,80,384]{2,1,0:T(8,128)(2,1)S(1)} all-gather(bf16[4,80,384]{2,1,0:T(8,128)(2,1)S(1)} %constant_dynamic-slice_fusion), channel_id=3, replica_groups=mesh['zh'=4,'zl'=4,'yh'=2,'yl'=4,'x'=4,'c'=2] {'x'}, dimensions={0}, use_global_device_ids=true | all-gather | bytes 1228800 | tf_op jit(solution)/shard_map/all_gather | solution.py:168
  82.2 13.8 %collective-permute-start = (bf16[4,4,80,384]{3,2,1,0:T(8,128)(2,1)S(1)}, bf16[4,4,80,384]{3,2,1,0:T(8,128)(2,1)S(1)}, u32[]{:S(2)}, u32[]{:S(2)}) collective-permute-start(bf16[4,4,80,384]{3,2,1,0:T(8,128)(2,1)S(1)} %bitcast.10), channel_id=1, source_target_pairs={{0,1},{1,0},{2,3},{3,2},{4,5},{5,4},{6,7},{7,6},{8,9},{9,8},{10,11... | collective-permute-start | bytes 2949128 | tf_op jit(solution)/shard_map/ppermute | solution.py:170
  96.0 2.2 %collective-permute-done.refs_3_ = bf16[4,4,80,384]{3,2,1,0:T(8,128)(2,1)S(1)} collective-permute-done((bf16[4,4,80,384]{3,2,1,0:T(8,128)(2,1)S(1)}, bf16[4,4,80,384]{3,2,1,0:T(8,128)(2,1)S(1)}, u32[]{:S(2)}, u32[]{:S(2)}) %collective-permute-start) | collective-permute-done | bytes 983072 | tf_op jit(solution)/shard_map/ppermute | solution.py:170
  98.1 14.7 %all-to-all-done = bf16[32,24,1280]{2,1,0:T(8,128)(2,1)} async-done(((bf16[32,24,1280]{2,1,0:T(8,128)(2,1)}), bf16[32,24,1280]{2,1,0:T(8,128)(2,1)}, u32[]{:S(2)}, u32[]{:S(2)}) %all-to-all-start) | async-done | bytes 1966112 | tf_op jit(solution)/shard_map/all_to_all | solution.py:149
  112.9 5.7 %expert_grads.1 = (f32[4,4,80,384]{3,2,1,0:T(8,128)S(1)}, bf16[4,4,80,384]{3,2,1,0:T(8,128)(2,1)S(1)}) custom-call(s32[1]{0:T(128)} %bitcast.refs_0_, bf16[768,1280]{1,0:T(8,128)(2,1)} %bitcast.3.refs_1_, bf16[4,4,80,384]{3,2,1,0:T(8,128)(2,1)S(1)} %bitcast.11, bf16[4,4,80,384]{3,2,1,0:T(8,128)(2,1)S(1)} %collective-permute-done.refs_3_), custom_call_target="tpu_custom_call" | custom-call | tf_op jit(solution)/shard_map/expert_grads/pallas_call | solution.py:173
  118.6 7.6 %collective-permute-start.1 = (bf16[4,4,80,384]{3,2,1,0:T(8,128)(2,1)S(1)}, bf16[4,4,80,384]{3,2,1,0:T(8,128)(2,1)S(1)}, u32[]{:S(2)}, u32[]{:S(2)}) collective-permute-start(bf16[4,4,80,384]{3,2,1,0:T(8,128)(2,1)S(1)} %get-tuple-element.8), channel_id=1, source_target_pairs={{0,1},{1,0},{2,3},{3,2},{4,5},{5,4},{6,7},{7,6},{8,9},{9,8},{10,11... | collective-permute-start | bytes 2949128 | tf_op jit(solution)/shard_map/ppermute | solution.py:189
  126.2 2.2 %collective-permute-done.1 = bf16[4,4,80,384]{3,2,1,0:T(8,128)(2,1)S(1)} collective-permute-done((bf16[4,4,80,384]{3,2,1,0:T(8,128)(2,1)S(1)}, bf16[4,4,80,384]{3,2,1,0:T(8,128)(2,1)S(1)}, u32[]{:S(2)}, u32[]{:S(2)}) %collective-permute-start.1) | collective-permute-done | bytes 983072 | tf_op jit(solution)/shard_map/ppermute | solution.py:189
  128.3 0.2 add_convert_fusion
  128.6 17.6 %all_to_all.25 = bf16[4,4,80,384]{3,2,1,0:T(8,128)(2,1)S(1)} all-to-all(bf16[4,4,80,384]{3,2,1,0:T(8,128)(2,1)S(1)} %add_convert_fusion), channel_id=1, replica_groups=mesh['zh'=4,'zl'=4,'yh'=2,'yl'=4,'x'=4,'c'=2] {'x'}, dimensions={0} | all-to-all | bytes 1966080 | tf_op jit(solution)/shard_map/all_to_all | solution.py:190
  146.2 0.2 reduce_sum.21
  146.4 12.3 %all_to_all.26 = bf16[4,80,384]{2,1,0:T(8,128)(2,1)S(1)} all-to-all(bf16[4,80,384]{2,1,0:T(8,128)(2,1)S(1)} %reduce_sum.21), channel_id=1, replica_groups=mesh['zh'=4,'zl'=4,'yh'=2,'yl'=4,'x'=4,'c'=2] {'yl'}, dimensions={0} | all-to-all | bytes 491520 | tf_op jit(solution)/shard_map/all_to_all | solution.py:192
  158.7 21.3 %all_to_all.27 = bf16[4,80,384]{2,1,0:T(8,128)(2,1)S(1)} all-to-all(bf16[4,80,384]{2,1,0:T(8,128)(2,1)S(1)} %all_to_all.26), channel_id=1, replica_groups=mesh['zh'=4,'zl'=4,'yh'=2,'yl'=4,'x'=4,'c'=2] {'zh'}, dimensions={0} | all-to-all | bytes 491520 | tf_op jit(solution)/shard_map/all_to_all | solution.py:193
  180.0 0.7 convert_reduce_fusion
  (10 shorter events, 0.0 us)
Async XLA Ops:
  0.0 51.7 %copy-start.1 = (bf16[128,2560]{1,0:T(8,128)(2,1)S(1)}, bf16[128,2560]{1,0:T(8,128)(2,1)}, u32[]{:S(2)}) copy-start(bf16[128,2560]{1,0:T(8,128)(2,1)} %refs_3_.1) | copy-start | bytes 1966084
  0.0 51.7 %copy-start = (bf16[128,2560]{1,0:T(8,128)(2,1)S(1)}, bf16[128,2560]{1,0:T(8,128)(2,1)}, u32[]{:S(2)}) copy-start(bf16[128,2560]{1,0:T(8,128)(2,1)} %refs_2_.1) | copy-start | bytes 1966084
  42.8 0.7 copy-start.2
  43.5 8.3 %copy-start.4 = (s32[128,1]{0,1:T(1,128)S(1)}, s32[128,1]{0,1:T(1,128)}, u32[]{:S(2)}) copy-start(s32[128,1]{0,1:T(1,128)} %param.11) | copy-start | bytes 1540
  43.5 8.3 %copy-start.5 = (f32[128]{0:T(128)S(1)}, f32[128]{0:T(128)}, u32[]{:S(2)}) copy-start(f32[128]{0:T(128)} %refs_1_.1) | copy-start | bytes 1540
  44.9 18.6 %all-to-all-start.1 = ((bf16[8,80,384]{2,1,0:T(8,128)(2,1)}), bf16[8,80,384]{2,1,0:T(8,128)(2,1)S(1)}, u32[]{:S(2)}, u32[]{:S(2)}) async-start(bf16[8,80,384]{2,1,0:T(8,128)(2,1)} %pick_slices.1), calls=%async_computation.1 | async-start | bytes 983040 | tf_op jit(solution)/shard_map/all_to_all | solution.py:165
  63.5 4.9 %copy-start.3 = (s32[32]{0:T(128)S(1)}, s32[32]{0:T(128)}, u32[]{:S(2)}) copy-start(s32[32]{0:T(128)} %seeds_ref.1) | copy-start | bytes 388
  63.5 49.4 %all-to-all-start = ((bf16[32,24,1280]{2,1,0:T(8,128)(2,1)}), bf16[32,24,1280]{2,1,0:T(8,128)(2,1)}, u32[]{:S(2)}, u32[]{:S(2)}) async-start(bf16[32,24,1280]{2,1,0:T(8,128)(2,1)} %bitcast.2), calls=%async_computation | async-start | bytes 3932160 | tf_op jit(solution)/shard_map/all_to_all | solution.py:149
  82.2 16.0 %collective-permute-start = (bf16[4,4,80,384]{3,2,1,0:T(8,128)(2,1)S(1)}, bf16[4,4,80,384]{3,2,1,0:T(8,128)(2,1)S(1)}, u32[]{:S(2)}, u32[]{:S(2)}) collective-permute-start(bf16[4,4,80,384]{3,2,1,0:T(8,128)(2,1)S(1)} %bitcast.10), channel_id=1, source_target_pairs={{0,1},{1,0},{2,3},{3,2},{4,5},{5,4},{6,7},{7,6},{8,9},{9,8},{10,11... | collective-permute-start | bytes 2949128 | tf_op jit(solution)/shard_map/ppermute | solution.py:170
  118.6 9.8 %collective-permute-start.1 = (bf16[4,4,80,384]{3,2,1,0:T(8,128)(2,1)S(1)}, bf16[4,4,80,384]{3,2,1,0:T(8,128)(2,1)S(1)}, u32[]{:S(2)}, u32[]{:S(2)}) collective-permute-start(bf16[4,4,80,384]{3,2,1,0:T(8,128)(2,1)S(1)} %get-tuple-element.8), channel_id=1, source_target_pairs={{0,1},{1,0},{2,3},{3,2},{4,5},{5,4},{6,7},{7,6},{8,9},{9,8},{10,11... | collective-permute-start | bytes 2949128 | tf_op jit(solution)/shard_map/ppermute | solution.py:189

commit v3 on v2

--- a/solution.py
+++ b/solution.py
@@ -65,7 +65,7 @@
 
 
 def expert_grads(
-    capacity, core_ref, arrived_ref, own_ref, other_ref, mine_ref, theirs_ref, weights, grads, sems
+    capacity, core_ref, arrived_ref, own_ref, other_ref, mine_ref, theirs_ref, weights, grads
 ):
     n_x, n_yl = own_ref.shape[:2]
     total, half = arrived_ref.shape
@@ -73,14 +73,9 @@
     hidden = weights.shape[-1] // 3
     features = 2 * half
     core = core_ref[0]
-    copies = []
     for x in range(n_x):
-        copies.append(pltpu.make_async_copy(own_ref.at[x], weights.at[:, x, core], sems.at[x]))
-        copies.append(
-            pltpu.make_async_copy(other_ref.at[x], weights.at[:, x, 1 - core], sems.at[n_x + x])
-        )
-    for copy in copies:
-        copy.start()
+        weights[:, x, core] = own_ref[x]
+        weights[:, x, 1 - core] = other_ref[x]
     within, column = iota((rows, total), 0), iota((rows, total), 1)
     source = (within * 10923) >> 16
     first = within + source * ((PIECES - 1) * capacity)
@@ -91,8 +86,6 @@
         return jnp.dot(chosen, arrived, preferred_element_type=jnp.float32).astype(jnp.bfloat16)
 
     x0, x1, g0, g1 = (sorted_rows(piece) for piece in range(PIECES))
-    for copy in copies:
-        copy.wait()
     flat = weights[...].reshape(features, 3 * hidden)
 
     def product(low, high, lanes):
@@ -176,12 +169,11 @@
             jax.ShapeDtypeStruct(half_shape, jnp.float32),
             jax.ShapeDtypeStruct(half_shape, bf16),
         ],
-        in_specs=[smem, vmem, anywhere, anywhere],
+        in_specs=[smem, vmem, vmem, vmem],
         out_specs=[vmem, vmem],
         scratch_shapes=[
             pltpu.VMEM((n_yl, n_x, n_c, block, width), bf16),
             pltpu.VMEM((n_yl, n_x, n_c, block, width), jnp.float32),
-            pltpu.SemaphoreType.DMA((2 * n_x,)),
         ],
         compiler_params=params,
         name="expert_grads",

time: 184 us -> 183 us (level)
  no operation moved by 1% of the time
where the time goes in v3:
time: 183 us; the launch traced here: 180 us
  blocking collectives  104 us (57%)
  starting transfers between devices  33.1 us (18%)
  waiting for transfers between devices  28.2 us (15%)
  Pallas kernels  9.05 us (5%)
  between operations  2.07 us (1%)
  other arithmetic  2 us (1%)
    all_gather x1, blocking collectives, on_device(): slices = lax.all_gather(own, ('zh', 'zl'), axis=0, tiled=False)  41.9 us
    all_to_all x1, blocking collectives, on_device(): lax.all_to_all(by_home, 'zh', split_axis=0, concat_axis=0, tiled=True)  21.2 us
    all_to_all x1, blocking collectives, on_device(): by_x = lax.all_to_all(pair, 'x', split_axis=0, concat_axis=0, tiled=True)  17.6 us
    all_to_all x1, waiting for transfers between devices, on_device(): lax.all_to_all(placed.reshape(experts, chunk, half), DISPATCH, split_axis...  14.7 us
    ppermute x1, starting transfers between devices, on_device(): other_rows = lax.ppermute(own_rows, 'c', swap)  13.8 us
    all_to_all x1, blocking collectives, on_device(): lax.all_to_all(row_sums, 'yl', split_axis=0, concat_axis=0, tiled=True)  12.3 us
    all_gather x1, blocking collectives, on_device(): own_rows = lax.all_gather(seeded, 'x', axis=0, tiled=False)  11.2 us
    all_to_all x1, waiting for transfers between devices, on_device(): lax.all_to_all(offered, ('yh', 'yl'), split_axis=0, concat_axis=0, tiled=...  9.11 us
  transfers between devices with their start and end apart: 4, of which 4 were waited for; matrix products, arithmetic and copies ran while one was open for 0% of the time, Pallas kernels for 1%

profile of v3, /device:TPU:1, one launch (start us, length us, event | category | flops | bytes accessed | tf_op | source)
XLA Modules:
  0.0 179.9 jit_solution(2096008808562974434)
XLA Ops:
  0.0 0.9 pad_maximum_fusion
  0.9 41.9 %all-gather = bf16[1280,384]{1,0:T(8,128)(2,1)S(1)} all-gather(bf16[80,384]{1,0:T(8,128)(2,1)S(1)} %pad_maximum_fusion), channel_id=2, replica_groups=mesh['zh'=4,'zl'=4,'yh'=2,'yl'=4,'x'=4,'c'=2] {'zh','zl'}, dimensions={0}, use_global_device_ids=true | all-gather | bytes 1044480 | tf_op jit(solution)/shard_map/all_gather | solution.py:148
  42.8 0.7 copy-done.2
  43.5 1.4 pick_slices.1
  44.9 6.8 %all-to-all-start.1 = ((bf16[8,80,384]{2,1,0:T(8,128)(2,1)}), bf16[8,80,384]{2,1,0:T(8,128)(2,1)S(1)}, u32[]{:S(2)}, u32[]{:S(2)}) async-start(bf16[8,80,384]{2,1,0:T(8,128)(2,1)} %pick_slices.1), calls=%async_computation.1 | async-start | bytes 983040 | tf_op jit(solution)/shard_map/all_to_all | solution.py:158
  51.7 0.0 copy-done.1
  51.7 0.0 copy-done
  51.7 2.6 %place_rows.1 = bf16[768,1280]{1,0:T(8,128)(2,1)} custom-call(s32[128]{0:T(128)S(1)} %bitcast.12, f32[128]{0:T(128)S(1)} %copy-done.5, bf16[128,2560]{1,0:T(8,128)(2,1)S(1)} %copy-done, bf16[128,2560]{1,0:T(8,128)(2,1)S(1)} %copy-done.1), custom_call_target="tpu_custom_call" | custom-call | tf_op jit(solution)/shard_map/place_rows/pallas_call | solution.py:134
  54.4 9.1 %all-to-all-done.1 = bf16[8,80,384]{2,1,0:T(8,128)(2,1)S(1)} async-done(((bf16[8,80,384]{2,1,0:T(8,128)(2,1)}), bf16[8,80,384]{2,1,0:T(8,128)(2,1)S(1)}, u32[]{:S(2)}, u32[]{:S(2)}) %all-to-all-start.1) | async-done | bytes 491552 | tf_op jit(solution)/shard_map/all_to_all | solution.py:158
  63.5 4.9 %all-to-all-start = ((bf16[32,24,1280]{2,1,0:T(8,128)(2,1)}), bf16[32,24,1280]{2,1,0:T(8,128)(2,1)}, u32[]{:S(2)}, u32[]{:S(2)}) async-start(bf16[32,24,1280]{2,1,0:T(8,128)(2,1)} %bitcast.2), calls=%async_computation | async-start | bytes 3932160 | tf_op jit(solution)/shard_map/all_to_all | solution.py:142
  68.4 0.6 dynamic_slice.6
  71.0 11.2 %all-gather.1 = bf16[16,80,384]{2,1,0:T(8,128)(2,1)S(1)} all-gather(bf16[4,80,384]{2,1,0:T(8,128)(2,1)S(1)} %constant_dynamic-slice_fusion), channel_id=3, replica_groups=mesh['zh'=4,'zl'=4,'yh'=2,'yl'=4,'x'=4,'c'=2] {'x'}, dimensions={0}, use_global_device_ids=true | all-gather | bytes 1228800 | tf_op jit(solution)/shard_map/all_gather | solution.py:161
  82.2 13.8 %collective-permute-start = (bf16[4,4,80,384]{3,2,1,0:T(8,128)(2,1)S(1)}, bf16[4,4,80,384]{3,2,1,0:T(8,128)(2,1)S(1)}, u32[]{:S(2)}, u32[]{:S(2)}) collective-permute-start(bf16[4,4,80,384]{3,2,1,0:T(8,128)(2,1)S(1)} %bitcast.10), channel_id=1, source_target_pairs={{0,1},{1,0},{2,3},{3,2},{4,5},{5,4},{6,7},{7,6},{8,9},{9,8},{10,11... | collective-permute-start | bytes 2949128 | tf_op jit(solution)/shard_map/ppermute | solution.py:163
  96.0 2.2 %collective-permute-done.refs_3_ = bf16[4,4,80,384]{3,2,1,0:T(8,128)(2,1)S(1)} collective-permute-done((bf16[4,4,80,384]{3,2,1,0:T(8,128)(2,1)S(1)}, bf16[4,4,80,384]{3,2,1,0:T(8,128)(2,1)S(1)}, u32[]{:S(2)}, u32[]{:S(2)}) %collective-permute-start) | collective-permute-done | bytes 983072 | tf_op jit(solution)/shard_map/ppermute | solution.py:163
  98.1 14.7 %all-to-all-done = bf16[32,24,1280]{2,1,0:T(8,128)(2,1)} async-done(((bf16[32,24,1280]{2,1,0:T(8,128)(2,1)}), bf16[32,24,1280]{2,1,0:T(8,128)(2,1)}, u32[]{:S(2)}, u32[]{:S(2)}) %all-to-all-start) | async-done | bytes 1966112 | tf_op jit(solution)/shard_map/all_to_all | solution.py:142
  112.9 5.0 %expert_grads.1 = (f32[4,4,80,384]{3,2,1,0:T(8,128)S(1)}, bf16[4,4,80,384]{3,2,1,0:T(8,128)(2,1)S(1)}) custom-call(s32[1]{0:T(128)} %bitcast.refs_0_, bf16[768,1280]{1,0:T(8,128)(2,1)} %bitcast.3.refs_1_, bf16[4,4,80,384]{3,2,1,0:T(8,128)(2,1)S(1)} %bitcast.11, bf16[4,4,80,384]{3,2,1,0:T(8,128)(2,1)S(1)} %collective-permute-done.refs_3_), custom_call_target="tpu_custom_call" | custom-call | tf_op jit(solution)/shard_map/expert_grads/pallas_call | solution.py:166
  117.9 7.6 %collective-permute-start.1 = (bf16[4,4,80,384]{3,2,1,0:T(8,128)(2,1)S(1)}, bf16[4,4,80,384]{3,2,1,0:T(8,128)(2,1)S(1)}, u32[]{:S(2)}, u32[]{:S(2)}) collective-permute-start(bf16[4,4,80,384]{3,2,1,0:T(8,128)(2,1)S(1)} %get-tuple-element.8), channel_id=1, source_target_pairs={{0,1},{1,0},{2,3},{3,2},{4,5},{5,4},{6,7},{7,6},{8,9},{9,8},{10,11... | collective-permute-start | bytes 2949128 | tf_op jit(solution)/shard_map/ppermute | solution.py:181
  125.5 2.2 %collective-permute-done.1 = bf16[4,4,80,384]{3,2,1,0:T(8,128)(2,1)S(1)} collective-permute-done((bf16[4,4,80,384]{3,2,1,0:T(8,128)(2,1)S(1)}, bf16[4,4,80,384]{3,2,1,0:T(8,128)(2,1)S(1)}, u32[]{:S(2)}, u32[]{:S(2)}) %collective-permute-start.1) | collective-permute-done | bytes 983072 | tf_op jit(solution)/shard_map/ppermute | solution.py:181
  127.7 0.2 add_convert_fusion
  127.9 17.6 %all_to_all.25 = bf16[4,4,80,384]{3,2,1,0:T(8,128)(2,1)S(1)} all-to-all(bf16[4,4,80,384]{3,2,1,0:T(8,128)(2,1)S(1)} %add_convert_fusion), channel_id=1, replica_groups=mesh['zh'=4,'zl'=4,'yh'=2,'yl'=4,'x'=4,'c'=2] {'x'}, dimensions={0} | all-to-all | bytes 1966080 | tf_op jit(solution)/shard_map/all_to_all | solution.py:182
  145.5 0.2 reduce_sum.21
  145.8 12.3 %all_to_all.26 = bf16[4,80,384]{2,1,0:T(8,128)(2,1)S(1)} all-to-all(bf16[4,80,384]{2,1,0:T(8,128)(2,1)S(1)} %reduce_sum.21), channel_id=1, replica_groups=mesh['zh'=4,'zl'=4,'yh'=2,'yl'=4,'x'=4,'c'=2] {'yl'}, dimensions={0} | all-to-all | bytes 491520 | tf_op jit(solution)/shard_map/all_to_all | solution.py:184
  158.0 21.2 %all_to_all.27 = bf16[4,80,384]{2,1,0:T(8,128)(2,1)S(1)} all-to-all(bf16[4,80,384]{2,1,0:T(8,128)(2,1)S(1)} %all_to_all.26), channel_id=1, replica_groups=mesh['zh'=4,'zl'=4,'yh'=2,'yl'=4,'x'=4,'c'=2] {'zh'}, dimensions={0} | all-to-all | bytes 491520 | tf_op jit(solution)/shard_map/all_to_all | solution.py:185
  179.2 0.7 convert_reduce_fusion
  (10 shorter events, 0.0 us)
Async XLA Ops:
  0.0 51.7 %copy-start.1 = (bf16[128,2560]{1,0:T(8,128)(2,1)S(1)}, bf16[128,2560]{1,0:T(8,128)(2,1)}, u32[]{:S(2)}) copy-start(bf16[128,2560]{1,0:T(8,128)(2,1)} %refs_3_.1) | copy-start | bytes 1966084
  0.0 51.7 %copy-start = (bf16[128,2560]{1,0:T(8,128)(2,1)S(1)}, bf16[128,2560]{1,0:T(8,128)(2,1)}, u32[]{:S(2)}) copy-start(bf16[128,2560]{1,0:T(8,128)(2,1)} %refs_2_.1) | copy-start | bytes 1966084
  42.8 0.7 copy-start.2
  43.5 8.3 %copy-start.4 = (s32[128,1]{0,1:T(1,128)S(1)}, s32[128,1]{0,1:T(1,128)}, u32[]{:S(2)}) copy-start(s32[128,1]{0,1:T(1,128)} %param.11) | copy-start | bytes 1540
  43.5 8.3 %copy-start.5 = (f32[128]{0:T(128)S(1)}, f32[128]{0:T(128)}, u32[]{:S(2)}) copy-start(f32[128]{0:T(128)} %refs_1_.1) | copy-start | bytes 1540
  44.9 18.6 %all-to-all-start.1 = ((bf16[8,80,384]{2,1,0:T(8,128)(2,1)}), bf16[8,80,384]{2,1,0:T(8,128)(2,1)S(1)}, u32[]{:S(2)}, u32[]{:S(2)}) async-start(bf16[8,80,384]{2,1,0:T(8,128)(2,1)} %pick_slices.1), calls=%async_computation.1 | async-start | bytes 983040 | tf_op jit(solution)/shard_map/all_to_all | solution.py:158
  63.5 4.9 %copy-start.3 = (s32[32]{0:T(128)S(1)}, s32[32]{0:T(128)}, u32[]{:S(2)}) copy-start(s32[32]{0:T(128)} %seeds_ref.1) | copy-start | bytes 388
  63.5 49.4 %all-to-all-start = ((bf16[32,24,1280]{2,1,0:T(8,128)(2,1)}), bf16[32,24,1280]{2,1,0:T(8,128)(2,1)}, u32[]{:S(2)}, u32[]{:S(2)}) async-start(bf16[32,24,1280]{2,1,0:T(8,128)(2,1)} %bitcast.2), calls=%async_computation | async-start | bytes 3932160 | tf_op jit(solution)/shard_map/all_to_all | solution.py:142
  82.2 16.0 %collective-permute-start = (bf16[4,4,80,384]{3,2,1,0:T(8,128)(2,1)S(1)}, bf16[4,4,80,384]{3,2,1,0:T(8,128)(2,1)S(1)}, u32[]{:S(2)}, u32[]{:S(2)}) collective-permute-start(bf16[4,4,80,384]{3,2,1,0:T(8,128)(2,1)S(1)} %bitcast.10), channel_id=1, source_target_pairs={{0,1},{1,0},{2,3},{3,2},{4,5},{5,4},{6,7},{7,6},{8,9},{9,8},{10,11... | collective-permute-start | bytes 2949128 | tf_op jit(solution)/shard_map/ppermute | solution.py:163
  117.9 9.8 %collective-permute-start.1 = (bf16[4,4,80,384]{3,2,1,0:T(8,128)(2,1)S(1)}, bf16[4,4,80,384]{3,2,1,0:T(8,128)(2,1)S(1)}, u32[]{:S(2)}, u32[]{:S(2)}) collective-permute-start(bf16[4,4,80,384]{3,2,1,0:T(8,128)(2,1)S(1)} %get-tuple-element.8), channel_id=1, source_target_pairs={{0,1},{1,0},{2,3},{3,2},{4,5},{5,4},{6,7},{7,6},{8,9},{9,8},{10,11... | collective-permute-start | bytes 2949128 | tf_op jit(solution)/shard_map/ppermute | solution.py:181

commit v4 on v3

--- a/solution.py
+++ b/solution.py
@@ -11,7 +11,7 @@
 SIZES = (4, 4, 2, 4, 4, 2)
 DISPATCH = ("yl", "zl", "yh")
 PIECES = 4
-VMEM_LIMIT = 48 * 1024 * 1024
+VMEM_LIMIT = 24 * 1024 * 1024
 
 
 def iota(shape, dim):
@@ -65,7 +65,7 @@
 
 
 def expert_grads(
-    capacity, core_ref, arrived_ref, own_ref, other_ref, mine_ref, theirs_ref, weights, grads
+    capacity, core_ref, arrived_ref, own_ref, other_ref, mine_ref, theirs_ref, weights
 ):
     n_x, n_yl = own_ref.shape[:2]
     total, half = arrived_ref.shape
@@ -104,14 +104,15 @@
     n_half = n_yl // 2
     blocks = (n_half, n_x, 2, weights.shape[3])
     for part, (rows_x, rows_g) in enumerate(((x0, g0), (x1, g1))):
-        at = slice(part * n_half, (part + 1) * n_half)
-        grads[at, :, :, :, : 2 * hidden] = contract_rows(rows_x, grad_pre).reshape(
-            blocks + (2 * hidden,)
-        )
-        grads[at, :, :, :, 2 * hidden :] = contract_rows(rows_g, mixed).reshape(blocks + (hidden,))
-    for x in range(n_x):
-        mine_ref[x] = grads[:, x, core]
-        theirs_ref[x] = grads[:, x, 1 - core].astype(jnp.bfloat16)
+        from_x = contract_rows(rows_x, grad_pre).reshape(blocks + (2 * hidden,))
+        from_g = contract_rows(rows_g, mixed).reshape(blocks + (hidden,))
+        both = jnp.concatenate([from_x, from_g], axis=-1)
+        for yl in range(n_half):
+            for x in range(n_x):
+                first, second = both[yl, x, 0], both[yl, x, 1]
+                to = (x, part * n_half + yl)
+                mine_ref[to] = jnp.where(core == 0, first, second)
+                theirs_ref[to] = jnp.where(core == 0, second, first).astype(jnp.bfloat16)
 
 
 def on_device(
@@ -173,7 +174,6 @@
         out_specs=[vmem, vmem],
         scratch_shapes=[
             pltpu.VMEM((n_yl, n_x, n_c, block, width), bf16),
-            pltpu.VMEM((n_yl, n_x, n_c, block, width), jnp.float32),
         ],
         compiler_params=params,
         name="expert_grads",

time: 183 us -> 181 us (0.989)
  Pallas kernels: 9.05 us -> 7.16 us
where the time goes in v4:
time: 181 us; the launch traced here: 179 us
  blocking collectives  105 us (58%)
  starting transfers between devices  32.3 us (18%)
  waiting for transfers between devices  28.3 us (16%)
  Pallas kernels  7.16 us (4%)
  local copies, waits for them, and re-layouts  2.59 us (1%)
  between operations  2.09 us (1%)
  other arithmetic  2.06 us (1%)
    all_gather x1, blocking collectives, on_device(): slices = lax.all_gather(own, ('zh', 'zl'), axis=0, tiled=False)  41.9 us
    all_to_all x1, blocking collectives, on_device(): lax.all_to_all(by_home, 'zh', split_axis=0, concat_axis=0, tiled=True)  22.7 us
    all_to_all x1, blocking collectives, on_device(): by_x = lax.all_to_all(pair, 'x', split_axis=0, concat_axis=0, tiled=True)  17.6 us
    all_to_all x1, waiting for transfers between devices, on_device(): lax.all_to_all(placed.reshape(experts, chunk, half), DISPATCH, split_axis...  14.7 us
    ppermute x1, starting transfers between devices, on_device(): other_rows = lax.ppermute(own_rows, 'c', swap)  13.9 us
    all_to_all x1, blocking collectives, on_device(): lax.all_to_all(row_sums, 'yl', split_axis=0, concat_axis=0, tiled=True)  11.5 us
    all_gather x1, blocking collectives, on_device(): own_rows = lax.all_gather(seeded, 'x', axis=0, tiled=False)  11.2 us
    all_to_all x1, waiting for transfers between devices, on_device(): lax.all_to_all(offered, ('yh', 'yl'), split_axis=0, concat_axis=0, tiled=...  9.11 us
  transfers between devices with their start and end apart: 4, of which 4 were waited for; matrix products, arithmetic and copies ran while one was open for 0% of the time, Pallas kernels for 1%

profile of v4, /device:TPU:1, one launch (start us, length us, event | category | flops | bytes accessed | tf_op | source)
XLA Modules:
  0.0 179.4 jit_solution(5855214321663136114)
XLA Ops:
  0.0 0.9 pad_maximum_fusion
  0.9 41.9 %all-gather = bf16[1280,384]{1,0:T(8,128)(2,1)S(1)} all-gather(bf16[80,384]{1,0:T(8,128)(2,1)S(1)} %pad_maximum_fusion), channel_id=2, replica_groups=mesh['zh'=4,'zl'=4,'yh'=2,'yl'=4,'x'=4,'c'=2] {'zh','zl'}, dimensions={0}, use_global_device_ids=true | all-gather | bytes 1044480 | tf_op jit(solution)/shard_map/all_gather | solution.py:149
  42.8 0.7 copy-done.3
  43.5 1.4 pick_slices.1
  44.9 6.8 %all-to-all-start.1 = ((bf16[8,80,384]{2,1,0:T(8,128)(2,1)}), bf16[8,80,384]{2,1,0:T(8,128)(2,1)S(1)}, u32[]{:S(2)}, u32[]{:S(2)}) async-start(bf16[8,80,384]{2,1,0:T(8,128)(2,1)} %pick_slices.1), calls=%async_computation.1 | async-start | bytes 983040 | tf_op jit(solution)/shard_map/all_to_all | solution.py:159
  51.7 0.0 copy-done.2
  51.7 1.3 place_rows.1
  53.1 1.3 copy-done
  54.4 9.1 %all-to-all-done.1 = bf16[8,80,384]{2,1,0:T(8,128)(2,1)S(1)} async-done(((bf16[8,80,384]{2,1,0:T(8,128)(2,1)}), bf16[8,80,384]{2,1,0:T(8,128)(2,1)S(1)}, u32[]{:S(2)}, u32[]{:S(2)}) %all-to-all-start.1) | async-done | bytes 491552 | tf_op jit(solution)/shard_map/all_to_all | solution.py:159
  63.5 4.1 %all-to-all-start = ((bf16[32,24,1280]{2,1,0:T(8,128)(2,1)}), bf16[32,24,1280]{2,1,0:T(8,128)(2,1)S(1)}, u32[]{:S(2)}, u32[]{:S(2)}) async-start(bf16[32,24,1280]{2,1,0:T(8,128)(2,1)} %bitcast.10), calls=%async_computation | async-start | bytes 3932160 | tf_op jit(solution)/shard_map/all_to_all | solution.py:143
  67.7 0.6 dynamic_slice.6
  70.2 11.2 %all-gather.1 = bf16[16,80,384]{2,1,0:T(8,128)(2,1)S(1)} all-gather(bf16[4,80,384]{2,1,0:T(8,128)(2,1)S(1)} %constant_dynamic-slice_fusion), channel_id=3, replica_groups=mesh['zh'=4,'zl'=4,'yh'=2,'yl'=4,'x'=4,'c'=2] {'x'}, dimensions={0}, use_global_device_ids=true | all-gather | bytes 1228800 | tf_op jit(solution)/shard_map/all_gather | solution.py:162
  81.4 13.9 %collective-permute-start = (bf16[4,4,80,384]{3,2,1,0:T(8,128)(2,1)S(1)}, bf16[4,4,80,384]{3,2,1,0:T(8,128)(2,1)}, u32[]{:S(2)}, u32[]{:S(2)}) collective-permute-start(bf16[4,4,80,384]{3,2,1,0:T(8,128)(2,1)S(1)} %bitcast.12), channel_id=1, source_target_pairs={{0,1},{1,0},{2,3},{3,2},{4,5},{5,4},{6,7},{7,6},{8,9},{9,8},{10,11... | collective-permute-start | bytes 2949128 | tf_op jit(solution)/shard_map/ppermute | solution.py:164
  95.3 2.3 %collective-permute-done.refs_3_ = bf16[4,4,80,384]{3,2,1,0:T(8,128)(2,1)} collective-permute-done((bf16[4,4,80,384]{3,2,1,0:T(8,128)(2,1)S(1)}, bf16[4,4,80,384]{3,2,1,0:T(8,128)(2,1)}, u32[]{:S(2)}, u32[]{:S(2)}) %collective-permute-start) | collective-permute-done | bytes 983072 | tf_op jit(solution)/shard_map/ppermute | solution.py:164
  97.6 14.7 %all-to-all-done = bf16[32,24,1280]{2,1,0:T(8,128)(2,1)S(1)} async-done(((bf16[32,24,1280]{2,1,0:T(8,128)(2,1)}), bf16[32,24,1280]{2,1,0:T(8,128)(2,1)S(1)}, u32[]{:S(2)}, u32[]{:S(2)}) %all-to-all-start) | async-done | bytes 1966112 | tf_op jit(solution)/shard_map/all_to_all | solution.py:143
  112.4 4.4 %expert_grads.1 = (f32[4,4,80,384]{3,2,1,0:T(8,128)S(1)}, bf16[4,4,80,384]{3,2,1,0:T(8,128)(2,1)S(1)}) custom-call(s32[1]{0:T(128)} %bitcast.refs_0_, bf16[768,1280]{1,0:T(8,128)(2,1)S(1)} %bitcast.9, bf16[4,4,80,384]{3,2,1,0:T(8,128)(2,1)S(1)} %bitcast.13, bf16[4,4,80,384]{3,2,1,0:T(8,128)(2,1)} %collective-permute-done.refs_3_), custom_call_target="tpu_custom_call" | custom-call | tf_op jit(solution)/shard_map/expert_grads/pallas_call | solution.py:167
  116.8 7.4 %collective-permute-start.1 = (bf16[4,4,80,384]{3,2,1,0:T(8,128)(2,1)S(1)}, bf16[4,4,80,384]{3,2,1,0:T(8,128)(2,1)S(1)}, u32[]{:S(2)}, u32[]{:S(2)}) collective-permute-start(bf16[4,4,80,384]{3,2,1,0:T(8,128)(2,1)S(1)} %get-tuple-element.8), channel_id=1, source_target_pairs={{0,1},{1,0},{2,3},{3,2},{4,5},{5,4},{6,7},{7,6},{8,9},{9,8},{10,11... | collective-permute-start | bytes 2949128 | tf_op jit(solution)/shard_map/ppermute | solution.py:181
  124.2 2.2 %collective-permute-done.1 = bf16[4,4,80,384]{3,2,1,0:T(8,128)(2,1)S(1)} collective-permute-done((bf16[4,4,80,384]{3,2,1,0:T(8,128)(2,1)S(1)}, bf16[4,4,80,384]{3,2,1,0:T(8,128)(2,1)S(1)}, u32[]{:S(2)}, u32[]{:S(2)}) %collective-permute-start.1) | collective-permute-done | bytes 983072 | tf_op jit(solution)/shard_map/ppermute | solution.py:181
  126.4 0.3 add_convert_fusion
  126.7 17.6 %all_to_all.25 = bf16[4,4,80,384]{3,2,1,0:T(8,128)(2,1)S(1)} all-to-all(bf16[4,4,80,384]{3,2,1,0:T(8,128)(2,1)S(1)} %add_convert_fusion), channel_id=1, replica_groups=mesh['zh'=4,'zl'=4,'yh'=2,'yl'=4,'x'=4,'c'=2] {'x'}, dimensions={0} | all-to-all | bytes 1966080 | tf_op jit(solution)/shard_map/all_to_all | solution.py:182
  144.3 0.2 reduce_sum.21
  144.6 11.5 %all_to_all.26 = bf16[4,80,384]{2,1,0:T(8,128)(2,1)S(1)} all-to-all(bf16[4,80,384]{2,1,0:T(8,128)(2,1)S(1)} %reduce_sum.21), channel_id=1, replica_groups=mesh['zh'=4,'zl'=4,'yh'=2,'yl'=4,'x'=4,'c'=2] {'yl'}, dimensions={0} | all-to-all | bytes 491520 | tf_op jit(solution)/shard_map/all_to_all | solution.py:184
  156.0 22.7 %all_to_all.27 = bf16[4,80,384]{2,1,0:T(8,128)(2,1)S(1)} all-to-all(bf16[4,80,384]{2,1,0:T(8,128)(2,1)S(1)} %all_to_all.26), channel_id=1, replica_groups=mesh['zh'=4,'zl'=4,'yh'=2,'yl'=4,'x'=4,'c'=2] {'zh'}, dimensions={0} | all-to-all | bytes 491520 | tf_op jit(solution)/shard_map/all_to_all | solution.py:185
  178.7 0.7 convert_reduce_fusion
  (12 shorter events, 0.1 us)
Async XLA Ops:
  0.0 51.7 %copy-start.2 = (bf16[128,2560]{1,0:T(8,128)(2,1)S(1)}, bf16[128,2560]{1,0:T(8,128)(2,1)}, u32[]{:S(2)}) copy-start(bf16[128,2560]{1,0:T(8,128)(2,1)} %refs_3_.1) | copy-start | bytes 1966084
  0.0 51.7 %copy-start.1 = (bf16[128,2560]{1,0:T(8,128)(2,1)S(1)}, bf16[128,2560]{1,0:T(8,128)(2,1)}, u32[]{:S(2)}) copy-start(bf16[128,2560]{1,0:T(8,128)(2,1)} %refs_2_.1) | copy-start | bytes 1966084
  42.8 0.7 copy-start.3
  43.5 8.3 %copy-start.5 = (s32[128,1]{0,1:T(1,128)S(1)}, s32[128,1]{0,1:T(1,128)}, u32[]{:S(2)}) copy-start(s32[128,1]{0,1:T(1,128)} %param.11) | copy-start | bytes 1540
  43.5 8.3 %copy-start.6 = (f32[128]{0:T(128)S(1)}, f32[128]{0:T(128)}, u32[]{:S(2)}) copy-start(f32[128]{0:T(128)} %refs_1_.1) | copy-start | bytes 1540
  44.9 18.6 %all-to-all-start.1 = ((bf16[8,80,384]{2,1,0:T(8,128)(2,1)}), bf16[8,80,384]{2,1,0:T(8,128)(2,1)S(1)}, u32[]{:S(2)}, u32[]{:S(2)}) async-start(bf16[8,80,384]{2,1,0:T(8,128)(2,1)} %pick_slices.1), calls=%async_computation.1 | async-start | bytes 983040 | tf_op jit(solution)/shard_map/all_to_all | solution.py:159
  53.1 1.3 copy-start
  63.5 4.2 %copy-start.4 = (s32[32]{0:T(128)S(1)}, s32[32]{0:T(128)}, u32[]{:S(2)}) copy-start(s32[32]{0:T(128)} %seeds_ref.1) | copy-start | bytes 388
  63.5 48.9 %all-to-all-start = ((bf16[32,24,1280]{2,1,0:T(8,128)(2,1)}), bf16[32,24,1280]{2,1,0:T(8,128)(2,1)S(1)}, u32[]{:S(2)}, u32[]{:S(2)}) async-start(bf16[32,24,1280]{2,1,0:T(8,128)(2,1)} %bitcast.10), calls=%async_computation | async-start | bytes 3932160 | tf_op jit(solution)/shard_map/all_to_all | solution.py:143
  81.4 16.2 %collective-permute-start = (bf16[4,4,80,384]{3,2,1,0:T(8,128)(2,1)S(1)}, bf16[4,4,80,384]{3,2,1,0:T(8,128)(2,1)}, u32[]{:S(2)}, u32[]{:S(2)}) collective-permute-start(bf16[4,4,80,384]{3,2,1,0:T(8,128)(2,1)S(1)} %bitcast.12), channel_id=1, source_target_pairs={{0,1},{1,0},{2,3},{3,2},{4,5},{5,4},{6,7},{7,6},{8,9},{9,8},{10,11... | collective-permute-start | bytes 2949128 | tf_op jit(solution)/shard_map/ppermute | solution.py:164
  116.8 9.6 %collective-permute-start.1 = (bf16[4,4,80,384]{3,2,1,0:T(8,128)(2,1)S(1)}, bf16[4,4,80,384]{3,2,1,0:T(8,128)(2,1)S(1)}, u32[]{:S(2)}, u32[]{:S(2)}) collective-permute-start(bf16[4,4,80,384]{3,2,1,0:T(8,128)(2,1)S(1)} %get-tuple-element.8), channel_id=1, source_target_pairs={{0,1},{1,0},{2,3},{3,2},{4,5},{5,4},{6,7},{7,6},{8,9},{9,8},{10,11... | collective-permute-start | bytes 2949128 | tf_op jit(solution)/shard_map/ppermute | solution.py:181

commit v5 on v4

--- a/solution.py
+++ b/solution.py
@@ -11,7 +11,7 @@
 SIZES = (4, 4, 2, 4, 4, 2)
 DISPATCH = ("yl", "zl", "yh")
 PIECES = 4
-VMEM_LIMIT = 24 * 1024 * 1024
+VMEM_LIMIT = 16 * 1024 * 1024
 
 
 def iota(shape, dim):
@@ -44,20 +44,16 @@
     out_ref[...] = out.astype(jnp.bfloat16)
 
 
-def pick_slices(zl_ref, seeds_ref, stack_ref, out_ref, sems):
+def pick_slices(seed_map_ref, stack_ref, out_ref, seeds_ref, sem):
     _, n_zl, n_yh, n_yl, _, _ = SIZES
-    copies = []
+    zl = lax.axis_index("zl")
+    copy = pltpu.make_async_copy(seed_map_ref, seeds_ref, sem)
+    copy.start()
+    copy.wait()
     for yh in range(n_yh):
         for yl in range(n_yl):
-            seed = seeds_ref[(yl * n_zl + zl_ref[0]) * n_yh + yh]
-            to = yh * n_yl + yl
-            copies.append(
-                pltpu.make_async_copy(stack_ref.at[seed // n_yh], out_ref.at[to], sems.at[to])
-            )
-    for copy in copies:
-        copy.start()
-    for copy in copies:
-        copy.wait()
+            seed = seeds_ref[(yl * n_zl + zl) * n_yh + yh]
+            out_ref[yh * n_yl + yl] = stack_ref[seed // n_yh]
 
 
 def contract_rows(first, second):
@@ -128,7 +124,6 @@
     chunk = PIECES * capacity
     vmem = pl.BlockSpec(memory_space=pltpu.VMEM)
     smem = pl.BlockSpec(memory_space=pltpu.SMEM)
-    anywhere = pl.BlockSpec(memory_space=pl.ANY)
     params = pltpu.CompilerParams(vmem_limit_bytes=VMEM_LIMIT)
     bf16 = jnp.bfloat16
 
@@ -144,18 +139,18 @@
         placed.reshape(experts, chunk, half), DISPATCH, split_axis=0, concat_axis=0, tiled=True
     ).reshape(experts * chunk, half)
 
-    zl, core = lax.axis_index("zl"), lax.axis_index("c")
+    core = lax.axis_index("c")
     own = jnp.concatenate([dense_gate, dense_up, dense_down_t], axis=1)
     slices = lax.all_gather(own, ("zh", "zl"), axis=0, tiled=False)
     offered = pl.pallas_call(
         pick_slices,
         out_shape=jax.ShapeDtypeStruct((n_yh * n_yl, block, width), bf16),
-        in_specs=[smem, smem, anywhere],
-        out_specs=anywhere,
-        scratch_shapes=[pltpu.SemaphoreType.DMA((n_yh * n_yl,))],
+        in_specs=[pl.BlockSpec(memory_space=pl.ANY), vmem],
+        out_specs=vmem,
+        scratch_shapes=[pltpu.SMEM(seed_map.shape, jnp.int32), pltpu.SemaphoreType.DMA],
         compiler_params=params,
         name="pick_slices",
-    )(zl.reshape(1), seed_map, slices)
+    )(seed_map, slices)
     sent = lax.all_to_all(offered, ("yh", "yl"), split_axis=0, concat_axis=0, tiled=True)
     my_seed = seed_map[lax.axis_index(DISPATCH)]
     seeded = lax.dynamic_slice_in_dim(sent, (my_seed % n_yh) * n_yl, n_yl, 0)

time: 181 us -> 182 us (level)
  waiting for transfers between devices: 28.3 us -> 26.4 us
    all_to_all x1, waiting for transfers between devices: 14.7 us -> 12.7 us  [on_device(): lax.all_to_all(placed.reshape(experts, chunk, half), DISPATCH, split_axis...]
  transfers between devices with their start and end apart: 4 -> 4, of which waited for: 4 -> 4; matrix products, arithmetic and copies ran while one was open for 0% -> 1% of each run, Pallas kernels for 1% -> 1%
where the time goes in v5:
time: 182 us; the launch traced here: 179 us
  blocking collectives  105 us (58%)
  starting transfers between devices  33.2 us (18%)
  waiting for transfers between devices  26.4 us (15%)
  Pallas kernels  7.18 us (4%)
  local copies, waits for them, and re-layouts  3.54 us (2%)
  between operations  2.09 us (1%)
  other arithmetic  2.04 us (1%)
    all_gather x1, blocking collectives, on_device(): slices = lax.all_gather(own, ('zh', 'zl'), axis=0, tiled=False)  41.9 us
    all_to_all x1, blocking collectives, on_device(): lax.all_to_all(by_home, 'zh', split_axis=0, concat_axis=0, tiled=True)  22.1 us
    all_to_all x1, blocking collectives, on_device(): by_x = lax.all_to_all(pair, 'x', split_axis=0, concat_axis=0, tiled=True)  17.6 us
    ppermute x1, starting transfers between devices, on_device(): other_rows = lax.ppermute(own_rows, 'c', swap)  13.9 us
    all_to_all x1, waiting for transfers between devices, on_device(): lax.all_to_all(placed.reshape(experts, chunk, half), DISPATCH, split_axis...  12.7 us
    all_to_all x1, blocking collectives, on_device(): lax.all_to_all(row_sums, 'yl', split_axis=0, concat_axis=0, tiled=True)  12 us
    all_gather x1, blocking collectives, on_device(): own_rows = lax.all_gather(seeded, 'x', axis=0, tiled=False)  11.2 us
    all_to_all x1, waiting for transfers between devices, on_device(): lax.all_to_all(offered, ('yh', 'yl'), split_axis=0, concat_axis=0, tiled=...  9.22 us
  transfers between devices with their start and end apart: 4, of which 4 were waited for; matrix products, arithmetic and copies ran while one was open for 1% of the time, Pallas kernels for 1%

profile of v5, /device:TPU:1, one launch (start us, length us, event | category | flops | bytes accessed | tf_op | source)
XLA Modules:
  0.0 179.3 jit_solution(16725048431578401861)
XLA Ops:
  0.0 0.9 pad_maximum_fusion
  0.9 41.9 %all-gather = bf16[1280,384]{1,0:T(8,128)(2,1)S(1)} all-gather(bf16[80,384]{1,0:T(8,128)(2,1)S(1)} %pad_maximum_fusion), channel_id=2, replica_groups=mesh['zh'=4,'zl'=4,'yh'=2,'yl'=4,'x'=4,'c'=2] {'zh','zl'}, dimensions={0}, use_global_device_ids=true | all-gather | bytes 1044480 | tf_op jit(solution)/shard_map/all_gather | solution.py:144
  42.8 0.7 copy-done.5
  43.5 1.4 pick_slices.1
  44.9 6.8 %all-to-all-start.1 = ((bf16[8,80,384]{2,1,0:T(8,128)(2,1)}), bf16[8,80,384]{2,1,0:T(8,128)(2,1)}, u32[]{:S(2)}, u32[]{:S(2)}) async-start(bf16[8,80,384]{2,1,0:T(8,128)(2,1)} %pick_slices.1), calls=%async_computation.1 | async-start | bytes 983040 | tf_op jit(solution)/shard_map/all_to_all | solution.py:154
  51.8 1.3 place_rows.1
  53.1 1.3 copy-done
  54.4 9.2 %all-to-all-done.1 = bf16[8,80,384]{2,1,0:T(8,128)(2,1)} async-done(((bf16[8,80,384]{2,1,0:T(8,128)(2,1)}), bf16[8,80,384]{2,1,0:T(8,128)(2,1)}, u32[]{:S(2)}, u32[]{:S(2)}) %all-to-all-start.1) | async-done | bytes 491552 | tf_op jit(solution)/shard_map/all_to_all | solution.py:154
  63.6 4.1 %all-to-all-start = ((bf16[32,24,1280]{2,1,0:T(8,128)(2,1)}), bf16[32,24,1280]{2,1,0:T(8,128)(2,1)S(1)}, u32[]{:S(2)}, u32[]{:S(2)}) async-start(bf16[32,24,1280]{2,1,0:T(8,128)(2,1)} %bitcast.9), calls=%async_computation | async-start | bytes 3932160 | tf_op jit(solution)/shard_map/all_to_all | solution.py:138
  67.8 0.6 dynamic_slice.6
  70.3 1.0 constant_dynamic-slice_fusion
  71.3 11.2 %all-gather.1 = bf16[16,80,384]{2,1,0:T(8,128)(2,1)S(1)} all-gather(bf16[4,80,384]{2,1,0:T(8,128)(2,1)S(1)} %constant_dynamic-slice_fusion), channel_id=3, replica_groups=mesh['zh'=4,'zl'=4,'yh'=2,'yl'=4,'x'=4,'c'=2] {'x'}, dimensions={0}, use_global_device_ids=true | all-gather | bytes 1228800 | tf_op jit(solution)/shard_map/all_gather | solution.py:157
  82.5 13.9 %collective-permute-start = (bf16[4,4,80,384]{3,2,1,0:T(8,128)(2,1)S(1)}, bf16[4,4,80,384]{3,2,1,0:T(8,128)(2,1)}, u32[]{:S(2)}, u32[]{:S(2)}) collective-permute-start(bf16[4,4,80,384]{3,2,1,0:T(8,128)(2,1)S(1)} %bitcast.11), channel_id=1, source_target_pairs={{0,1},{1,0},{2,3},{3,2},{4,5},{5,4},{6,7},{7,6},{8,9},{9,8},{10,11... | collective-permute-start | bytes 2949128 | tf_op jit(solution)/shard_map/ppermute | solution.py:159
  96.4 2.3 %collective-permute-done.refs_3_ = bf16[4,4,80,384]{3,2,1,0:T(8,128)(2,1)} collective-permute-done((bf16[4,4,80,384]{3,2,1,0:T(8,128)(2,1)S(1)}, bf16[4,4,80,384]{3,2,1,0:T(8,128)(2,1)}, u32[]{:S(2)}, u32[]{:S(2)}) %collective-permute-start) | collective-permute-done | bytes 983072 | tf_op jit(solution)/shard_map/ppermute | solution.py:159
  98.7 12.7 %all-to-all-done = bf16[32,24,1280]{2,1,0:T(8,128)(2,1)S(1)} async-done(((bf16[32,24,1280]{2,1,0:T(8,128)(2,1)}), bf16[32,24,1280]{2,1,0:T(8,128)(2,1)S(1)}, u32[]{:S(2)}, u32[]{:S(2)}) %all-to-all-start) | async-done | bytes 1966112 | tf_op jit(solution)/shard_map/all_to_all | solution.py:138
  111.4 4.4 %expert_grads.1 = (f32[4,4,80,384]{3,2,1,0:T(8,128)S(1)}, bf16[4,4,80,384]{3,2,1,0:T(8,128)(2,1)S(1)}) custom-call(s32[1]{0:T(128)} %bitcast.refs_0_, bf16[768,1280]{1,0:T(8,128)(2,1)S(1)} %bitcast.8, bf16[4,4,80,384]{3,2,1,0:T(8,128)(2,1)S(1)} %bitcast.12, bf16[4,4,80,384]{3,2,1,0:T(8,128)(2,1)} %collective-permute-done.refs_3_), custom_call_target="tpu_custom_call" | custom-call | tf_op jit(solution)/shard_map/expert_grads/pallas_call | solution.py:162
  115.9 8.3 %collective-permute-start.1 = (bf16[4,4,80,384]{3,2,1,0:T(8,128)(2,1)S(1)}, bf16[4,4,80,384]{3,2,1,0:T(8,128)(2,1)S(1)}, u32[]{:S(2)}, u32[]{:S(2)}) collective-permute-start(bf16[4,4,80,384]{3,2,1,0:T(8,128)(2,1)S(1)} %get-tuple-element.8), channel_id=1, source_target_pairs={{0,1},{1,0},{2,3},{3,2},{4,5},{5,4},{6,7},{7,6},{8,9},{9,8},{10,11... | collective-permute-start | bytes 2949128 | tf_op jit(solution)/shard_map/ppermute | solution.py:176
  124.2 2.2 %collective-permute-done.1 = bf16[4,4,80,384]{3,2,1,0:T(8,128)(2,1)S(1)} collective-permute-done((bf16[4,4,80,384]{3,2,1,0:T(8,128)(2,1)S(1)}, bf16[4,4,80,384]{3,2,1,0:T(8,128)(2,1)S(1)}, u32[]{:S(2)}, u32[]{:S(2)}) %collective-permute-start.1) | collective-permute-done | bytes 983072 | tf_op jit(solution)/shard_map/ppermute | solution.py:176
  126.3 0.3 add_convert_fusion
  126.6 17.6 %all_to_all.25 = bf16[4,4,80,384]{3,2,1,0:T(8,128)(2,1)S(1)} all-to-all(bf16[4,4,80,384]{3,2,1,0:T(8,128)(2,1)S(1)} %add_convert_fusion), channel_id=1, replica_groups=mesh['zh'=4,'zl'=4,'yh'=2,'yl'=4,'x'=4,'c'=2] {'x'}, dimensions={0} | all-to-all | bytes 1966080 | tf_op jit(solution)/shard_map/all_to_all | solution.py:177
  144.2 0.2 reduce_sum.21
  144.5 12.0 %all_to_all.26 = bf16[4,80,384]{2,1,0:T(8,128)(2,1)S(1)} all-to-all(bf16[4,80,384]{2,1,0:T(8,128)(2,1)S(1)} %reduce_sum.21), channel_id=1, replica_groups=mesh['zh'=4,'zl'=4,'yh'=2,'yl'=4,'x'=4,'c'=2] {'yl'}, dimensions={0} | all-to-all | bytes 491520 | tf_op jit(solution)/shard_map/all_to_all | solution.py:179
  156.5 22.1 %all_to_all.27 = bf16[4,80,384]{2,1,0:T(8,128)(2,1)S(1)} all-to-all(bf16[4,80,384]{2,1,0:T(8,128)(2,1)S(1)} %all_to_all.26), channel_id=1, replica_groups=mesh['zh'=4,'zl'=4,'yh'=2,'yl'=4,'x'=4,'c'=2] {'zh'}, dimensions={0} | all-to-all | bytes 491520 | tf_op jit(solution)/shard_map/all_to_all | solution.py:180
  178.6 0.7 convert_reduce_fusion
  (12 shorter events, 0.0 us)
Async XLA Ops:
  0.0 51.7 %copy-start.3 = (s32[128,1]{0,1:T(1,128)S(1)}, s32[128,1]{0,1:T(1,128)}, u32[]{:S(2)}) copy-start(s32[128,1]{0,1:T(1,128)} %param.11) | copy-start | bytes 1540
  0.0 51.7 %copy-start.4 = (f32[128]{0:T(128)S(1)}, f32[128]{0:T(128)}, u32[]{:S(2)}) copy-start(f32[128]{0:T(128)} %refs_1_.1) | copy-start | bytes 1540
  0.0 51.7 %copy-start.2 = (bf16[128,2560]{1,0:T(8,128)(2,1)S(1)}, bf16[128,2560]{1,0:T(8,128)(2,1)}, u32[]{:S(2)}) copy-start(bf16[128,2560]{1,0:T(8,128)(2,1)} %refs_3_.1) | copy-start | bytes 1966084
  0.0 51.8 %copy-start.1 = (bf16[128,2560]{1,0:T(8,128)(2,1)S(1)}, bf16[128,2560]{1,0:T(8,128)(2,1)}, u32[]{:S(2)}) copy-start(bf16[128,2560]{1,0:T(8,128)(2,1)} %refs_2_.1) | copy-start | bytes 1966084
  42.8 0.7 copy-start.5
  44.9 18.7 %all-to-all-start.1 = ((bf16[8,80,384]{2,1,0:T(8,128)(2,1)}), bf16[8,80,384]{2,1,0:T(8,128)(2,1)}, u32[]{:S(2)}, u32[]{:S(2)}) async-start(bf16[8,80,384]{2,1,0:T(8,128)(2,1)} %pick_slices.1), calls=%async_computation.1 | async-start | bytes 983040 | tf_op jit(solution)/shard_map/all_to_all | solution.py:154
  53.1 1.3 copy-start
  63.6 4.2 %copy-start.6 = (s32[32]{0:T(128)S(1)}, s32[32]{0:T(128)}, u32[]{:S(2)}) copy-start(s32[32]{0:T(128)} %seed_map_ref.1) | copy-start | bytes 388
  63.6 47.8 %all-to-all-start = ((bf16[32,24,1280]{2,1,0:T(8,128)(2,1)}), bf16[32,24,1280]{2,1,0:T(8,128)(2,1)S(1)}, u32[]{:S(2)}, u32[]{:S(2)}) async-start(bf16[32,24,1280]{2,1,0:T(8,128)(2,1)} %bitcast.9), calls=%async_computation | async-start | bytes 3932160 | tf_op jit(solution)/shard_map/all_to_all | solution.py:138
  82.5 16.2 %collective-permute-start = (bf16[4,4,80,384]{3,2,1,0:T(8,128)(2,1)S(1)}, bf16[4,4,80,384]{3,2,1,0:T(8,128)(2,1)}, u32[]{:S(2)}, u32[]{:S(2)}) collective-permute-start(bf16[4,4,80,384]{3,2,1,0:T(8,128)(2,1)S(1)} %bitcast.11), channel_id=1, source_target_pairs={{0,1},{1,0},{2,3},{3,2},{4,5},{5,4},{6,7},{7,6},{8,9},{9,8},{10,11... | collective-permute-start | bytes 2949128 | tf_op jit(solution)/shard_map/ppermute | solution.py:159
  115.9 10.5 %collective-permute-start.1 = (bf16[4,4,80,384]{3,2,1,0:T(8,128)(2,1)S(1)}, bf16[4,4,80,384]{3,2,1,0:T(8,128)(2,1)S(1)}, u32[]{:S(2)}, u32[]{:S(2)}) collective-permute-start(bf16[4,4,80,384]{3,2,1,0:T(8,128)(2,1)S(1)} %get-tuple-element.8), channel_id=1, source_target_pairs={{0,1},{1,0},{2,3},{3,2},{4,5},{5,4},{6,7},{7,6},{8,9},{9,8},{10,11... | collective-permute-start | bytes 2949128 | tf_op jit(solution)/shard_map/ppermute | solution.py:176
